TPU v7x, 512 devices: a whole 4x4x16 slice. The times are simulated.
512 devices in a mesh: seq: 128 (over y, z, core), head: 4 (over x).
Axes of the slice: x: 4, y: 4, z: 16, core: 2. Of those that a mesh axis runs over, the one named last changes fastest.
Arguments:
- query_rows: bfloat16 [16384, 2048], P('seq', 'head'), may hold values from -5 to 5
- key_rows: bfloat16 [16384, 2048], P('seq', 'head'), may hold values from -5 to 5
- value_rows: bfloat16 [16384, 2048], P('seq', 'head'), may hold values from -6 to 6
- out_weight: bfloat16 [2048, 2048], P('head'), may hold values from -0.125 to 0.125
Outputs:
- layer_output: bfloat16 [16384, 2048], P(('seq', 'head'))
All inputs are finite; a program needn't handle non-finite values.
Results may differ from a plain program's by a relative error of at most 0.0053.
Values may be sent and summed in bfloat16 or wider, within the bound.
A program may use at most 128 MiB of HBM per device.

v0:
```python
import math

import jax
import jax.numpy as jnp
from jax import lax
from jax.sharding import PartitionSpec as P

HEAD_DIM = 128
SEG0 = 1024
LEVELS = 5


very_low = -1e30


def from_partner(value, axis, stride):
    mask = 2**stride
    pairs = [(source, source ^ mask) for source in range(lax.axis_size(axis))]
    return lax.ppermute(value, axis, pairs)


def select_rows(matrix, picker, step_rate):
    rows_dev = matrix.shape[0]
    heads_here = picker.shape[1]
    shaped = matrix.reshape(rows_dev // step_rate, step_rate, heads_here, HEAD_DIM)
    picked = jnp.einsum("arhd,rh->ahd", shaped, picker, preferred_element_type=jnp.float32)
    return picked.astype(jnp.bfloat16)


def spread_rows(selected, onehot, fill_value):
    if selected.ndim == 2:
        expanded = jnp.where(onehot[None, :, :], selected[:, None, :], fill_value)
        return expanded.reshape(-1, selected.shape[1])
    expanded = jnp.where(onehot[None, :, :, None], selected[:, None, :, :], fill_value)
    return expanded.reshape(-1, selected.shape[1], selected.shape[2])


def level_parts(q_sel, q_places, key_buffer, value_buffer, key_places):
    score_scale = 1.0 / math.sqrt(HEAD_DIM)
    scores = (
        jnp.einsum("ahd,khd->hak", q_sel, key_buffer, preferred_element_type=jnp.float32)
        * score_scale
    )
    allowed = key_places.T[:, None, :] <= q_places.T[:, :, None]
    masked = jnp.where(allowed, scores, very_low)
    peak_score = jnp.max(masked, axis=2)
    weights = jnp.where(allowed, jnp.exp(masked - peak_score[:, :, None]), 0.0)
    denominator = jnp.sum(weights, axis=2)
    numerator = jnp.einsum(
        "hak,khd->ahd",
        weights.astype(jnp.bfloat16),
        value_buffer,
        preferred_element_type=jnp.float32,
    )
    return (peak_score.T, denominator.T, numerator)


def trade(buffers, bit_number):
    return from_partner((buffers[0], buffers[1]), "seq", bit_number)


def extend_owners(owners, bit_number):
    return jnp.concatenate([owners, jnp.bitwise_xor(owners, jnp.int32(1 << bit_number))], axis=0)


def per_device(query_rows, key_rows, value_rows, out_weight):
    rows_dev = query_rows.shape[0]
    heads_here = query_rows.shape[1] // HEAD_DIM
    seq_count = lax.axis_size("seq")
    seq_here = lax.axis_index("seq")
    seq_start = seq_here * rows_dev
    head_ids = lax.axis_index("head") * heads_here + jnp.arange(heads_here, dtype=jnp.int32)
    level_data = []
    for level_index in range(LEVELS):
        step_rate = 2**level_index
        offsets = head_ids % step_rate
        onehot = jnp.arange(step_rate, dtype=jnp.int32)[:, None] == offsets[None, :]
        picker = onehot.astype(jnp.bfloat16)
        q_sel = select_rows(query_rows, picker, step_rate)
        k_sel = select_rows(key_rows, picker, step_rate)
        v_sel = select_rows(value_rows, picker, step_rate)
        pattern = (
            jnp.arange(rows_dev // step_rate, dtype=jnp.int32)[:, None] * step_rate
            + offsets[None, :]
        )
        places = seq_start + pattern
        group_size = min(SEG0 * step_rate // rows_dev, seq_count)
        bit_count = group_size.bit_length() - 1
        owners = jnp.reshape(seq_here, (1,))
        level_data.append([onehot, q_sel, places, k_sel, v_sel, owners, bit_count, pattern])
    for entry in level_data:
        bit_list = list(range(entry[6]))
        for bit_number in bit_list:
            other_keys, other_values = trade((entry[3], entry[4]), bit_number)
            entry[3] = jnp.concatenate([entry[3], other_keys], axis=0)
            entry[4] = jnp.concatenate([entry[4], other_values], axis=0)
            entry[5] = extend_owners(entry[5], bit_number)
    for level_index in range(LEVELS):
        onehot, q_sel, q_places, key_buffer, value_buffer, owners, bit_count, pattern = level_data[
            level_index
        ]
        key_places = (owners[:, None, None] * rows_dev + pattern[None, :, :]).reshape(
            -1, heads_here
        )
        peak_score, denominator, numerator = level_parts(
            q_sel, q_places, key_buffer, value_buffer, key_places
        )
        full_peak = spread_rows(peak_score, onehot, very_low)
        full_denom = spread_rows(denominator, onehot, 0.0)
        full_numer = spread_rows(numerator, onehot, 0.0)
        if level_index == 0:
            run_peak, run_denom, run_numer = (full_peak, full_denom, full_numer)
        else:
            new_peak = jnp.maximum(run_peak, full_peak)
            old_factor = jnp.exp(run_peak - new_peak)
            new_factor = jnp.exp(full_peak - new_peak)
            run_denom = run_denom * old_factor + full_denom * new_factor
            run_numer = run_numer * old_factor[:, :, None] + full_numer * new_factor[:, :, None]
            run_peak = new_peak
    attention = (
        (run_numer / run_denom[:, :, None])
        .astype(jnp.bfloat16)
        .reshape(rows_dev, heads_here * HEAD_DIM)
    )
    summed = lax.psum_scatter(
        jnp.dot(attention, out_weight, preferred_element_type=jnp.float32),
        "head",
        scatter_dimension=0,
        tiled=True,
    )
    return summed.astype(jnp.bfloat16)


def solution(mesh):
    in_specs = (P("seq", "head"), P("seq", "head"), P("seq", "head"), P("head", None))
    out_specs = P(("seq", "head"), None)
    return jax.shard_map(
        per_device, mesh=mesh, in_specs=in_specs, out_specs=out_specs, check_vma=False
    )
```

profile of v0, /device:TPU:17, one launch (start us, length us, event | category | flops | bytes accessed | tf_op | source)
XLA Modules:
  0.0 628.0 jit_solution(14955573177940272367)
XLA Ops:
  9.0 2.6 collective-permute-start.30
  17.6 2.4 collective-permute-start.19
  26.1 2.4 collective-permute-start.43
  98.7 2.1 collective-permute-start.36
  102.8 2.4 collective-permute-start.6
  110.6 3.5 collective-permute-start.44
  116.2 2.4 collective-permute-start.37
  120.7 3.8 collective-permute-start.3
  128.5 3.3 collective-permute-start.31
  135.5 2.0 collective-permute-start.25
  140.1 4.9 collective-permute-start.45
  146.6 4.0 collective-permute-start.38
  154.9 3.5 collective-permute-start.15
  158.5 3.8 collective-permute-start.32
  162.4 2.3 collective-permute-start.26
  165.6 8.8 %collective-permute-start.46 = (bf16[64,4,128]{2,0,1:T(8,128)(2,1)S(1)}, bf16[64,4,128]{2,0,1:T(8,128)(2,1)S(1)}, u32[]{:S(2)}, u32[]{:S(2)}) collective-permute-start(bf16[64,4,128]{2,0,1:T(8,128)(2,1)S(1)} %pad_maximum_fusion.21), channel_id=1, source_target_pairs={{0,32},{4,36},{8,40},{12,44},{16,48},{20,52},{24,56},{28,60},{32,0... | collective-permute-start | bytes 196616 | tf_op jit(solution)/shard_map/ppermute | solution.py:19
  183.3 3.4 collective-permute-start.11
  187.4 3.8 collective-permute-start.21
  192.0 2.3 collective-permute-start.16
  194.4 7.3 %collective-permute-start.33 = (bf16[128,4,128]{2,0,1:T(8,128)(2,1)S(1)}, bf16[128,4,128]{2,0,1:T(8,128)(2,1)S(1)}, u32[]{:S(2)}, u32[]{:S(2)}) collective-permute-start(bf16[128,4,128]{2,0,1:T(8,128)(2,1)S(1)} %pad_maximum_fusion.15), channel_id=1, source_target_pairs={{0,32},{4,36},{8,40},{12,44},{16,48},{20,52},{24,56},{28,60},{32,0... | collective-permute-start | bytes 393224 | tf_op jit(solution)/shard_map/ppermute | solution.py:19
  203.7 11.9 %collective-permute-start.47 = (bf16[128,4,128]{2,0,1:T(8,128)(2,1)S(1)}, bf16[128,4,128]{2,0,1:T(8,128)(2,1)S(1)}, u32[]{:S(2)}, u32[]{:S(2)}) collective-permute-start(bf16[128,4,128]{2,0,1:T(8,128)(2,1)S(1)} %get-tuple-element.70), channel_id=1, source_target_pairs={{0,64},{4,68},{8,72},{12,76},{16,80},{20,84},{24,88},{28,92},{32,9... | collective-permute-start | bytes 393224 | tf_op jit(solution)/shard_map/ppermute | solution.py:19
  215.7 2.1 collective-permute-start.40
  218.6 2.5 collective-permute-start.4
  223.4 2.8 collective-permute-start.1
  227.0 20.7 %collective-permute-done.27 = bf16[128,4,128]{2,0,1:T(8,128)(2,1)S(1)} collective-permute-done((bf16[128,4,128]{2,0,1:T(8,128)(2,1)S(1)}, bf16[128,4,128]{2,0,1:T(8,128)(2,1)S(1)}, u32[]{:S(2)}, u32[]{:S(2)}) %collective-permute-start.27) | collective-permute-done | bytes 131104 | tf_op jit(solution)/shard_map/ppermute | solution.py:19
  250.4 4.2 collective-permute-start.12
  255.4 5.1 collective-permute-start.22
  261.4 4.1 collective-permute-start.17
  265.5 7.9 %collective-permute-start.34 = (bf16[256,4,128]{2,0,1:T(8,128)(2,1)S(1)}, bf16[256,4,128]{2,0,1:T(8,128)(2,1)S(1)}, u32[]{:S(2)}, u32[]{:S(2)}) collective-permute-start(bf16[256,4,128]{2,0,1:T(8,128)(2,1)S(1)} %get-tuple-element.48), channel_id=1, source_target_pairs={{0,64},{4,68},{8,72},{12,76},{16,80},{20,84},{24,88},{28,92},{32,9... | collective-permute-start | bytes 786440 | tf_op jit(solution)/shard_map/ppermute | solution.py:19
  274.3 6.1 collective-permute-start.28
  280.5 11.7 %collective-permute-done.12 = bf16[256,4,128]{2,0,1:T(8,128)(2,1)S(1)} collective-permute-done((bf16[256,4,128]{2,0,1:T(8,128)(2,1)S(1)}, bf16[256,4,128]{2,0,1:T(8,128)(2,1)S(1)}, u32[]{:S(2)}, u32[]{:S(2)}) %collective-permute-start.12) | collective-permute-done | bytes 262176 | tf_op jit(solution)/shard_map/ppermute | solution.py:19
  292.1 2.9 collective-permute-start.48
  295.2 2.4 collective-permute-start.41
  298.5 10.3 %collective-permute-done.17 = bf16[256,4,128]{2,0,1:T(8,128)(2,1)S(1)} collective-permute-done((bf16[256,4,128]{2,0,1:T(8,128)(2,1)S(1)}, bf16[256,4,128]{2,0,1:T(8,128)(2,1)S(1)}, u32[]{:S(2)}, u32[]{:S(2)}) %collective-permute-start.17) | collective-permute-done | bytes 262176 | tf_op jit(solution)/shard_map/ppermute | solution.py:19
  308.7 25.0 %collective-permute-start.5 = (bf16[512,4,128]{2,0,1:T(8,128)(2,1)S(1)}, bf16[512,4,128]{2,0,1:T(8,128)(2,1)S(1)}, u32[]{:S(2)}, u32[]{:S(2)}) collective-permute-start(bf16[512,4,128]{2,0,1:T(8,128)(2,1)S(1)} %pad_maximum_fusion.1), channel_id=1, source_target_pairs={{0,16},{4,20},{8,24},{12,28},{16,0},{20,4},{24,8},{28,12},{32,48},... | collective-permute-start | bytes 1572872 | tf_op jit(solution)/shard_map/ppermute | solution.py:19
  334.7 14.0 %collective-permute-start.2 = (bf16[512,4,128]{0,2,1:T(8,128)(2,1)}, bf16[512,4,128]{0,2,1:T(8,128)(2,1)}, u32[]{:S(2)}, u32[]{:S(2)}) collective-permute-start(bf16[512,4,128]{0,2,1:T(8,128)(2,1)} %pad_maximum_fusion), channel_id=1, source_target_pairs={{0,16},{4,20},{8,24},{12,28},{16,0},{20,4},{24,8},{28,12},{32,48},... | collective-permute-start | bytes 1572872 | tf_op jit(solution)/shard_map/ppermute | solution.py:19
  352.4 7.3 %collective-permute-start.13 = (bf16[512,4,128]{2,0,1:T(8,128)(2,1)S(1)}, bf16[512,4,128]{2,0,1:T(8,128)(2,1)S(1)}, u32[]{:S(2)}, u32[]{:S(2)}) collective-permute-start(bf16[512,4,128]{2,0,1:T(8,128)(2,1)S(1)} %pad_maximum_fusion.3), channel_id=1, source_target_pairs={{0,32},{4,36},{8,40},{12,44},{16,48},{20,52},{24,56},{28,60},{32,0... | collective-permute-start | bytes 1572872 | tf_op jit(solution)/shard_map/ppermute | solution.py:19
  360.5 7.4 %collective-permute-start.23 = (bf16[512,4,128]{2,0,1:T(8,128)(2,1)}, bf16[512,4,128]{2,0,1:T(8,128)(2,1)}, u32[]{:S(2)}, u32[]{:S(2)}) collective-permute-start(bf16[512,4,128]{2,0,1:T(8,128)(2,1)} %get-tuple-element.36), channel_id=1, source_target_pairs={{0,64},{4,68},{8,72},{12,76},{16,80},{20,84},{24,88},{28,92},{32,9... | collective-permute-start | bytes 1572872 | tf_op jit(solution)/shard_map/ppermute | solution.py:19
  368.8 93.6 %collective-permute-done.5 = bf16[512,4,128]{2,0,1:T(8,128)(2,1)S(1)} collective-permute-done((bf16[512,4,128]{2,0,1:T(8,128)(2,1)S(1)}, bf16[512,4,128]{2,0,1:T(8,128)(2,1)S(1)}, u32[]{:S(2)}, u32[]{:S(2)}) %collective-permute-start.5) | collective-permute-done | bytes 524320 | tf_op jit(solution)/shard_map/ppermute | solution.py:19
  462.4 8.8 %collective-permute-start.18 = (bf16[512,4,128]{2,0,1:T(8,128)(2,1)}, bf16[512,4,128]{2,0,1:T(8,128)(2,1)}, u32[]{:S(2)}, u32[]{:S(2)}) collective-permute-start(bf16[512,4,128]{2,0,1:T(8,128)(2,1)} %get-tuple-element.40), channel_id=1, source_target_pairs={{0,64},{4,68},{8,72},{12,76},{16,80},{20,84},{24,88},{28,92},{32,9... | collective-permute-start | bytes 1572872 | tf_op jit(solution)/shard_map/ppermute | solution.py:19
  474.0 2.9 collective-permute-start.35
  479.8 2.6 collective-permute-start.29
  484.3 13.0 %collective-permute-done.18 = bf16[512,4,128]{2,0,1:T(8,128)(2,1)} collective-permute-done((bf16[512,4,128]{2,0,1:T(8,128)(2,1)}, bf16[512,4,128]{2,0,1:T(8,128)(2,1)}, u32[]{:S(2)}, u32[]{:S(2)}) %collective-permute-start.18) | collective-permute-done | bytes 524320 | tf_op jit(solution)/shard_map/ppermute | solution.py:19
  503.0 4.9 collective-permute-start.42
  510.7 2.0 constant_dynamic-update-slice_fusion.43
  524.1 2.5 fusion.6
  537.8 2.5 fusion.51
  540.3 79.2 %reduce-scatter.2.cloned.1.call-done = f32[32,2048]{1,0:T(8,128)} async-done(((f32[128,2048]{1,0:T(8,128)}), f32[32,2048]{1,0:T(8,128)}) %reduce-scatter.2.cloned.1.call-update) | async-done | bytes 262160 | tf_op jit(solution)/shard_map/reduce_scatter | solution.py:125
  (430 shorter events, 181.8 us)
Async XLA Ops:
  6.5 613.0 %reduce-scatter.2.cloned.1.call-start = ((), (), s32[]{:S(2)}) async-start(), calls=%async_computation.1 | async-start | bytes 1310720 | tf_op jit(solution)/shard_map/reduce_scatter | solution.py:125
  9.0 97.6 %collective-permute-start.30 = (bf16[16,4,128]{2,0,1:T(8,128)(2,1)}, bf16[16,4,128]{2,0,1:T(8,128)(2,1)}, u32[]{:S(2)}, u32[]{:S(2)}) collective-permute-start(bf16[16,4,128]{2,0,1:T(8,128)(2,1)} %get-tuple-element.6), channel_id=1, source_target_pairs={{0,4},{4,0},{8,12},{12,8},{16,20},{20,16},{24,28},{28,24},{32,36},... | collective-permute-start | bytes 49160 | tf_op jit(solution)/shard_map/ppermute | solution.py:19
  13.2 97.4 %collective-permute-start.24 = (bf16[16,4,128]{2,0,1:T(8,128)(2,1)S(1)}, bf16[16,4,128]{2,0,1:T(8,128)(2,1)}, u32[]{:S(2)}, u32[]{:S(2)}) collective-permute-start(bf16[16,4,128]{2,0,1:T(8,128)(2,1)S(1)} %get-tuple-element.33), channel_id=1, source_target_pairs={{0,4},{4,0},{8,12},{12,8},{16,20},{20,16},{24,28},{28,24},{32,36},... | collective-permute-start | bytes 49160 | tf_op jit(solution)/shard_map/ppermute | solution.py:19
  17.6 108.2 %collective-permute-start.19 = (bf16[32,4,128]{2,0,1:T(8,128)(2,1)}, bf16[32,4,128]{2,0,1:T(8,128)(2,1)}, u32[]{:S(2)}, u32[]{:S(2)}) collective-permute-start(bf16[32,4,128]{2,0,1:T(8,128)(2,1)} %get-tuple-element.10), channel_id=1, source_target_pairs={{0,4},{4,0},{8,12},{12,8},{16,20},{20,16},{24,28},{28,24},{32,36},... | collective-permute-start | bytes 98312 | tf_op jit(solution)/shard_map/ppermute | solution.py:19
  21.8 106.7 %collective-permute-start.14 = (bf16[32,4,128]{2,0,1:T(8,128)(2,1)}, bf16[32,4,128]{2,0,1:T(8,128)(2,1)}, u32[]{:S(2)}, u32[]{:S(2)}) collective-permute-start(bf16[32,4,128]{2,0,1:T(8,128)(2,1)} %get-tuple-element.27), channel_id=1, source_target_pairs={{0,4},{4,0},{8,12},{12,8},{16,20},{20,16},{24,28},{28,24},{32,36},... | collective-permute-start | bytes 98312 | tf_op jit(solution)/shard_map/ppermute | solution.py:19
  26.1 72.6 %collective-permute-start.43 = (bf16[8,4,128]{2,0,1:T(8,128)(2,1)}, bf16[8,4,128]{2,0,1:T(8,128)(2,1)}, u32[]{:S(2)}, u32[]{:S(2)}) collective-permute-start(bf16[8,4,128]{2,0,1:T(8,128)(2,1)} %get-tuple-element.12), channel_id=1, source_target_pairs={{0,4},{4,0},{8,12},{12,8},{16,20},{20,16},{24,28},{28,24},{32,36},... | collective-permute-start | bytes 24584 | tf_op jit(solution)/shard_map/ppermute | solution.py:19
  102.8 52.1 %collective-permute-start.6 = (bf16[64,4,128]{2,0,1:T(8,128)(2,1)}, bf16[64,4,128]{2,0,1:T(8,128)(2,1)S(1)}, u32[]{:S(2)}, u32[]{:S(2)}) collective-permute-start(bf16[64,4,128]{2,0,1:T(8,128)(2,1)} %get-tuple-element.29), channel_id=1, source_target_pairs={{0,4},{4,0},{8,12},{12,8},{16,20},{20,16},{24,28},{28,24},{32,36},... | collective-permute-start | bytes 196616 | tf_op jit(solution)/shard_map/ppermute | solution.py:19
  106.6 51.9 %collective-permute-start.10 = (bf16[64,4,128]{2,0,1:T(8,128)(2,1)}, bf16[64,4,128]{2,0,1:T(8,128)(2,1)S(1)}, u32[]{:S(2)}, u32[]{:S(2)}) collective-permute-start(bf16[64,4,128]{2,0,1:T(8,128)(2,1)} %get-tuple-element.8), channel_id=1, source_target_pairs={{0,4},{4,0},{8,12},{12,8},{16,20},{20,16},{24,28},{28,24},{32,36},... | collective-permute-start | bytes 196616 | tf_op jit(solution)/shard_map/ppermute | solution.py:19
  110.6 5.6 collective-permute-start.44
  120.7 71.3 %collective-permute-start.3 = (bf16[128,4,128]{2,0,1:T(8,128)(2,1)S(1)}, bf16[128,4,128]{2,0,1:T(8,128)(2,1)S(1)}, u32[]{:S(2)}, u32[]{:S(2)}) collective-permute-start(bf16[128,4,128]{2,0,1:T(8,128)(2,1)S(1)} %copy.45), channel_id=1, source_target_pairs={{0,4},{4,0},{8,12},{12,8},{16,20},{20,16},{24,28},{28,24},{32,36},... | collective-permute-start | bytes 393224 | tf_op jit(solution)/shard_map/ppermute | solution.py:19
  125.8 68.5 %collective-permute-start = (bf16[128,4,128]{0,2,1:T(8,128)(2,1)S(1)}, bf16[128,4,128]{0,2,1:T(8,128)(2,1)S(1)}, u32[]{:S(2)}, u32[]{:S(2)}) collective-permute-start(bf16[128,4,128]{0,2,1:T(8,128)(2,1)S(1)} %bitcast.312), channel_id=1, source_target_pairs={{0,4},{4,0},{8,12},{12,8},{16,20},{20,16},{24,28},{28,24},{32,36},... | collective-permute-start | bytes 393224 | tf_op jit(solution)/shard_map/ppermute | solution.py:19
  128.5 6.9 %collective-permute-start.31 = (bf16[32,4,128]{2,0,1:T(8,128)(2,1)S(1)}, bf16[32,4,128]{2,0,1:T(8,128)(2,1)S(1)}, u32[]{:S(2)}, u32[]{:S(2)}) collective-permute-start(bf16[32,4,128]{2,0,1:T(8,128)(2,1)S(1)} %pad_maximum_fusion.23), channel_id=1, source_target_pairs={{0,8},{4,12},{8,0},{12,4},{16,24},{20,28},{24,16},{28,20},{32,40},... | collective-permute-start | bytes 98312 | tf_op jit(solution)/shard_map/ppermute | solution.py:19
  140.1 6.5 %collective-permute-start.45 = (bf16[32,4,128]{2,0,1:T(8,128)(2,1)S(1)}, bf16[32,4,128]{2,0,1:T(8,128)(2,1)S(1)}, u32[]{:S(2)}, u32[]{:S(2)}) collective-permute-start(bf16[32,4,128]{2,0,1:T(8,128)(2,1)S(1)} %pad_maximum_fusion.25), channel_id=1, source_target_pairs={{0,16},{4,20},{8,24},{12,28},{16,0},{20,4},{24,8},{28,12},{32,48},... | collective-permute-start | bytes 98312 | tf_op jit(solution)/shard_map/ppermute | solution.py:19
  146.6 5.7 collective-permute-start.38
  152.3 10.1 %collective-permute-start.20 = (bf16[64,4,128]{2,0,1:T(8,128)(2,1)S(1)}, bf16[64,4,128]{2,0,1:T(8,128)(2,1)S(1)}, u32[]{:S(2)}, u32[]{:S(2)}) collective-permute-start(bf16[64,4,128]{2,0,1:T(8,128)(2,1)S(1)} %pad_maximum_fusion.17), channel_id=1, source_target_pairs={{0,8},{4,12},{8,0},{12,4},{16,24},{20,28},{24,16},{28,20},{32,40},... | collective-permute-start | bytes 196616 | tf_op jit(solution)/shard_map/ppermute | solution.py:19
  154.9 10.6 %collective-permute-start.15 = (bf16[64,4,128]{2,0,1:T(8,128)(2,1)S(1)}, bf16[64,4,128]{2,0,1:T(8,128)(2,1)S(1)}, u32[]{:S(2)}, u32[]{:S(2)}) collective-permute-start(bf16[64,4,128]{2,0,1:T(8,128)(2,1)S(1)} %pad_maximum_fusion.16), channel_id=1, source_target_pairs={{0,8},{4,12},{8,0},{12,4},{16,24},{20,28},{24,16},{28,20},{32,40},... | collective-permute-start | bytes 196616 | tf_op jit(solution)/shard_map/ppermute | solution.py:19
  158.5 18.1 %collective-permute-start.32 = (bf16[64,4,128]{2,0,1:T(8,128)(2,1)S(1)}, bf16[64,4,128]{2,0,1:T(8,128)(2,1)S(1)}, u32[]{:S(2)}, u32[]{:S(2)}) collective-permute-start(bf16[64,4,128]{2,0,1:T(8,128)(2,1)S(1)} %pad_maximum_fusion.19), channel_id=1, source_target_pairs={{0,16},{4,20},{8,24},{12,28},{16,0},{20,4},{24,8},{28,12},{32,48},... | collective-permute-start | bytes 196616 | tf_op jit(solution)/shard_map/ppermute | solution.py:19
  162.4 17.5 %collective-permute-start.26 = (bf16[64,4,128]{2,0,1:T(8,128)(2,1)S(1)}, bf16[64,4,128]{2,0,1:T(8,128)(2,1)S(1)}, u32[]{:S(2)}, u32[]{:S(2)}) collective-permute-start(bf16[64,4,128]{2,0,1:T(8,128)(2,1)S(1)} %pad_maximum_fusion.18), channel_id=1, source_target_pairs={{0,16},{4,20},{8,24},{12,28},{16,0},{20,4},{24,8},{28,12},{32,48},... | collective-permute-start | bytes 196616 | tf_op jit(solution)/shard_map/ppermute | solution.py:19
  165.6 17.7 %collective-permute-start.46 = (bf16[64,4,128]{2,0,1:T(8,128)(2,1)S(1)}, bf16[64,4,128]{2,0,1:T(8,128)(2,1)S(1)}, u32[]{:S(2)}, u32[]{:S(2)}) collective-permute-start(bf16[64,4,128]{2,0,1:T(8,128)(2,1)S(1)} %pad_maximum_fusion.21), channel_id=1, source_target_pairs={{0,32},{4,36},{8,40},{12,44},{16,48},{20,52},{24,56},{28,60},{32,0... | collective-permute-start | bytes 196616 | tf_op jit(solution)/shard_map/ppermute | solution.py:19
  176.6 10.8 %collective-permute-start.39 = (bf16[64,4,128]{2,0,1:T(8,128)(2,1)S(1)}, bf16[64,4,128]{2,0,1:T(8,128)(2,1)S(1)}, u32[]{:S(2)}, u32[]{:S(2)}) collective-permute-start(bf16[64,4,128]{2,0,1:T(8,128)(2,1)S(1)} %pad_maximum_fusion.20), channel_id=1, source_target_pairs={{0,32},{4,36},{8,40},{12,44},{16,48},{20,52},{24,56},{28,60},{32,0... | collective-permute-start | bytes 196616 | tf_op jit(solution)/shard_map/ppermute | solution.py:19
  179.9 21.7 %collective-permute-start.7 = (bf16[128,4,128]{2,0,1:T(8,128)(2,1)S(1)}, bf16[128,4,128]{2,0,1:T(8,128)(2,1)S(1)}, u32[]{:S(2)}, u32[]{:S(2)}) collective-permute-start(bf16[128,4,128]{2,0,1:T(8,128)(2,1)S(1)} %pad_maximum_fusion.10), channel_id=1, source_target_pairs={{0,8},{4,12},{8,0},{12,4},{16,24},{20,28},{24,16},{28,20},{32,40},... | collective-permute-start | bytes 393224 | tf_op jit(solution)/shard_map/ppermute | solution.py:19
  183.3 20.3 %collective-permute-start.11 = (bf16[128,4,128]{2,0,1:T(8,128)(2,1)S(1)}, bf16[128,4,128]{2,0,1:T(8,128)(2,1)S(1)}, u32[]{:S(2)}, u32[]{:S(2)}) collective-permute-start(bf16[128,4,128]{2,0,1:T(8,128)(2,1)S(1)} %pad_maximum_fusion.11), channel_id=1, source_target_pairs={{0,8},{4,12},{8,0},{12,4},{16,24},{20,28},{24,16},{28,20},{32,40},... | collective-permute-start | bytes 393224 | tf_op jit(solution)/shard_map/ppermute | solution.py:19
  187.4 28.3 %collective-permute-start.21 = (bf16[128,4,128]{2,0,1:T(8,128)(2,1)S(1)}, bf16[128,4,128]{2,0,1:T(8,128)(2,1)S(1)}, u32[]{:S(2)}, u32[]{:S(2)}) collective-permute-start(bf16[128,4,128]{2,0,1:T(8,128)(2,1)S(1)} %pad_maximum_fusion.13), channel_id=1, source_target_pairs={{0,16},{4,20},{8,24},{12,28},{16,0},{20,4},{24,8},{28,12},{32,48},... | collective-permute-start | bytes 393224 | tf_op jit(solution)/shard_map/ppermute | solution.py:19
  192.0 26.6 %collective-permute-start.16 = (bf16[128,4,128]{2,0,1:T(8,128)(2,1)S(1)}, bf16[128,4,128]{2,0,1:T(8,128)(2,1)S(1)}, u32[]{:S(2)}, u32[]{:S(2)}) collective-permute-start(bf16[128,4,128]{2,0,1:T(8,128)(2,1)S(1)} %pad_maximum_fusion.12), channel_id=1, source_target_pairs={{0,16},{4,20},{8,24},{12,28},{16,0},{20,4},{24,8},{28,12},{32,48},... | collective-permute-start | bytes 393224 | tf_op jit(solution)/shard_map/ppermute | solution.py:19
  194.4 29.0 %collective-permute-start.33 = (bf16[128,4,128]{2,0,1:T(8,128)(2,1)S(1)}, bf16[128,4,128]{2,0,1:T(8,128)(2,1)S(1)}, u32[]{:S(2)}, u32[]{:S(2)}) collective-permute-start(bf16[128,4,128]{2,0,1:T(8,128)(2,1)S(1)} %pad_maximum_fusion.15), channel_id=1, source_target_pairs={{0,32},{4,36},{8,40},{12,44},{16,48},{20,52},{24,56},{28,60},{32,0... | collective-permute-start | bytes 393224 | tf_op jit(solution)/shard_map/ppermute | solution.py:19
  201.7 46.0 %collective-permute-start.27 = (bf16[128,4,128]{2,0,1:T(8,128)(2,1)S(1)}, bf16[128,4,128]{2,0,1:T(8,128)(2,1)S(1)}, u32[]{:S(2)}, u32[]{:S(2)}) collective-permute-start(bf16[128,4,128]{2,0,1:T(8,128)(2,1)S(1)} %pad_maximum_fusion.14), channel_id=1, source_target_pairs={{0,32},{4,36},{8,40},{12,44},{16,48},{20,52},{24,56},{28,60},{32,0... | collective-permute-start | bytes 393224 | tf_op jit(solution)/shard_map/ppermute | solution.py:19
  203.7 46.8 %collective-permute-start.47 = (bf16[128,4,128]{2,0,1:T(8,128)(2,1)S(1)}, bf16[128,4,128]{2,0,1:T(8,128)(2,1)S(1)}, u32[]{:S(2)}, u32[]{:S(2)}) collective-permute-start(bf16[128,4,128]{2,0,1:T(8,128)(2,1)S(1)} %get-tuple-element.70), channel_id=1, source_target_pairs={{0,64},{4,68},{8,72},{12,76},{16,80},{20,84},{24,88},{28,92},{32,9... | collective-permute-start | bytes 393224 | tf_op jit(solution)/shard_map/ppermute | solution.py:19
  215.7 39.8 %collective-permute-start.40 = (bf16[128,4,128]{2,0,1:T(8,128)(2,1)S(1)}, bf16[128,4,128]{2,0,1:T(8,128)(2,1)S(1)}, u32[]{:S(2)}, u32[]{:S(2)}) collective-permute-start(bf16[128,4,128]{2,0,1:T(8,128)(2,1)S(1)} %get-tuple-element.79), channel_id=1, source_target_pairs={{0,64},{4,68},{8,72},{12,76},{16,80},{20,84},{24,88},{28,92},{32,9... | collective-permute-start | bytes 393224 | tf_op jit(solution)/shard_map/ppermute | solution.py:19
  218.6 42.8 %collective-permute-start.4 = (bf16[256,4,128]{2,0,1:T(8,128)(2,1)S(1)}, bf16[256,4,128]{2,0,1:T(8,128)(2,1)S(1)}, u32[]{:S(2)}, u32[]{:S(2)}) collective-permute-start(bf16[256,4,128]{2,0,1:T(8,128)(2,1)S(1)} %pad_maximum_fusion.5), channel_id=1, source_target_pairs={{0,8},{4,12},{8,0},{12,4},{16,24},{20,28},{24,16},{28,20},{32,40},... | collective-permute-start | bytes 786440 | tf_op jit(solution)/shard_map/ppermute | solution.py:19
  223.4 42.1 %collective-permute-start.1 = (bf16[256,4,128]{0,2,1:T(8,128)(2,1)S(1)}, bf16[256,4,128]{0,2,1:T(8,128)(2,1)S(1)}, u32[]{:S(2)}, u32[]{:S(2)}) collective-permute-start(bf16[256,4,128]{0,2,1:T(8,128)(2,1)S(1)} %pad_maximum_fusion.4), channel_id=1, source_target_pairs={{0,8},{4,12},{8,0},{12,4},{16,24},{20,28},{24,16},{28,20},{32,40},... | collective-permute-start | bytes 786440 | tf_op jit(solution)/shard_map/ppermute | solution.py:19
  247.7 26.6 %collective-permute-start.8 = (bf16[256,4,128]{2,0,1:T(8,128)(2,1)S(1)}, bf16[256,4,128]{2,0,1:T(8,128)(2,1)S(1)}, u32[]{:S(2)}, u32[]{:S(2)}) collective-permute-start(bf16[256,4,128]{2,0,1:T(8,128)(2,1)S(1)} %pad_maximum_fusion.6), channel_id=1, source_target_pairs={{0,16},{4,20},{8,24},{12,28},{16,0},{20,4},{24,8},{28,12},{32,48},... | collective-permute-start | bytes 786440 | tf_op jit(solution)/shard_map/ppermute | solution.py:19
  250.4 41.7 %collective-permute-start.12 = (bf16[256,4,128]{2,0,1:T(8,128)(2,1)S(1)}, bf16[256,4,128]{2,0,1:T(8,128)(2,1)S(1)}, u32[]{:S(2)}, u32[]{:S(2)}) collective-permute-start(bf16[256,4,128]{2,0,1:T(8,128)(2,1)S(1)} %pad_maximum_fusion.7), channel_id=1, source_target_pairs={{0,16},{4,20},{8,24},{12,28},{16,0},{20,4},{24,8},{28,12},{32,48},... | collective-permute-start | bytes 786440 | tf_op jit(solution)/shard_map/ppermute | solution.py:19
  255.4 39.8 %collective-permute-start.22 = (bf16[256,4,128]{2,0,1:T(8,128)(2,1)S(1)}, bf16[256,4,128]{2,0,1:T(8,128)(2,1)S(1)}, u32[]{:S(2)}, u32[]{:S(2)}) collective-permute-start(bf16[256,4,128]{2,0,1:T(8,128)(2,1)S(1)} %pad_maximum_fusion.9), channel_id=1, source_target_pairs={{0,32},{4,36},{8,40},{12,44},{16,48},{20,52},{24,56},{28,60},{32,0... | collective-permute-start | bytes 786440 | tf_op jit(solution)/shard_map/ppermute | solution.py:19
  261.4 47.3 %collective-permute-start.17 = (bf16[256,4,128]{2,0,1:T(8,128)(2,1)S(1)}, bf16[256,4,128]{2,0,1:T(8,128)(2,1)S(1)}, u32[]{:S(2)}, u32[]{:S(2)}) collective-permute-start(bf16[256,4,128]{2,0,1:T(8,128)(2,1)S(1)} %pad_maximum_fusion.8), channel_id=1, source_target_pairs={{0,32},{4,36},{8,40},{12,44},{16,48},{20,52},{24,56},{28,60},{32,0... | collective-permute-start | bytes 786440 | tf_op jit(solution)/shard_map/ppermute | solution.py:19
  265.5 69.1 %collective-permute-start.34 = (bf16[256,4,128]{2,0,1:T(8,128)(2,1)S(1)}, bf16[256,4,128]{2,0,1:T(8,128)(2,1)S(1)}, u32[]{:S(2)}, u32[]{:S(2)}) collective-permute-start(bf16[256,4,128]{2,0,1:T(8,128)(2,1)S(1)} %get-tuple-element.48), channel_id=1, source_target_pairs={{0,64},{4,68},{8,72},{12,76},{16,80},{20,84},{24,88},{28,92},{32,9... | collective-permute-start | bytes 786440 | tf_op jit(solution)/shard_map/ppermute | solution.py:19
  274.3 75.3 %collective-permute-start.28 = (bf16[256,4,128]{2,0,1:T(8,128)(2,1)S(1)}, bf16[256,4,128]{2,0,1:T(8,128)(2,1)S(1)}, u32[]{:S(2)}, u32[]{:S(2)}) collective-permute-start(bf16[256,4,128]{2,0,1:T(8,128)(2,1)S(1)} %get-tuple-element.58), channel_id=1, source_target_pairs={{0,64},{4,68},{8,72},{12,76},{16,80},{20,84},{24,88},{28,92},{32,9... | collective-permute-start | bytes 786440 | tf_op jit(solution)/shard_map/ppermute | solution.py:19
  292.1 60.3 %collective-permute-start.48 = (bf16[256,4,128]{2,0,1:T(8,128)(2,1)S(1)}, bf16[256,4,128]{2,0,1:T(8,128)(2,1)S(1)}, u32[]{:S(2)}, u32[]{:S(2)}) collective-permute-start(bf16[256,4,128]{2,0,1:T(8,128)(2,1)S(1)} %get-tuple-element.53), channel_id=1, source_target_pairs={{0,128},{4,132},{8,136},{12,140},{16,144},{20,148},{24,152},{28,15... | collective-permute-start | bytes 786440 | tf_op jit(solution)/shard_map/ppermute | solution.py:19
  295.2 65.3 %collective-permute-start.41 = (bf16[256,4,128]{2,0,1:T(8,128)(2,1)S(1)}, bf16[256,4,128]{2,0,1:T(8,128)(2,1)S(1)}, u32[]{:S(2)}, u32[]{:S(2)}) collective-permute-start(bf16[256,4,128]{2,0,1:T(8,128)(2,1)S(1)} %get-tuple-element.61), channel_id=1, source_target_pairs={{0,128},{4,132},{8,136},{12,140},{16,144},{20,148},{24,152},{28,15... | collective-permute-start | bytes 786440 | tf_op jit(solution)/shard_map/ppermute | solution.py:19
  308.7 153.7 %collective-permute-start.5 = (bf16[512,4,128]{2,0,1:T(8,128)(2,1)S(1)}, bf16[512,4,128]{2,0,1:T(8,128)(2,1)S(1)}, u32[]{:S(2)}, u32[]{:S(2)}) collective-permute-start(bf16[512,4,128]{2,0,1:T(8,128)(2,1)S(1)} %pad_maximum_fusion.1), channel_id=1, source_target_pairs={{0,16},{4,20},{8,24},{12,28},{16,0},{20,4},{24,8},{28,12},{32,48},... | collective-permute-start | bytes 1572872 | tf_op jit(solution)/shard_map/ppermute | solution.py:19
  334.7 189.4 %collective-permute-start.2 = (bf16[512,4,128]{0,2,1:T(8,128)(2,1)}, bf16[512,4,128]{0,2,1:T(8,128)(2,1)}, u32[]{:S(2)}, u32[]{:S(2)}) collective-permute-start(bf16[512,4,128]{0,2,1:T(8,128)(2,1)} %pad_maximum_fusion), channel_id=1, source_target_pairs={{0,16},{4,20},{8,24},{12,28},{16,0},{20,4},{24,8},{28,12},{32,48},... | collective-permute-start | bytes 1572872 | tf_op jit(solution)/shard_map/ppermute | solution.py:19
  349.6 124.4 %collective-permute-start.9 = (bf16[512,4,128]{2,0,1:T(8,128)(2,1)S(1)}, bf16[512,4,128]{2,0,1:T(8,128)(2,1)S(1)}, u32[]{:S(2)}, u32[]{:S(2)}) collective-permute-start(bf16[512,4,128]{2,0,1:T(8,128)(2,1)S(1)} %pad_maximum_fusion.2), channel_id=1, source_target_pairs={{0,32},{4,36},{8,40},{12,44},{16,48},{20,52},{24,56},{28,60},{32,0... | collective-permute-start | bytes 1572872 | tf_op jit(solution)/shard_map/ppermute | solution.py:19
  352.4 127.3 %collective-permute-start.13 = (bf16[512,4,128]{2,0,1:T(8,128)(2,1)S(1)}, bf16[512,4,128]{2,0,1:T(8,128)(2,1)S(1)}, u32[]{:S(2)}, u32[]{:S(2)}) collective-permute-start(bf16[512,4,128]{2,0,1:T(8,128)(2,1)S(1)} %pad_maximum_fusion.3), channel_id=1, source_target_pairs={{0,32},{4,36},{8,40},{12,44},{16,48},{20,52},{24,56},{28,60},{32,0... | collective-permute-start | bytes 1572872 | tf_op jit(solution)/shard_map/ppermute | solution.py:19
  360.5 142.4 %collective-permute-start.23 = (bf16[512,4,128]{2,0,1:T(8,128)(2,1)}, bf16[512,4,128]{2,0,1:T(8,128)(2,1)}, u32[]{:S(2)}, u32[]{:S(2)}) collective-permute-start(bf16[512,4,128]{2,0,1:T(8,128)(2,1)} %get-tuple-element.36), channel_id=1, source_target_pairs={{0,64},{4,68},{8,72},{12,76},{16,80},{20,84},{24,88},{28,92},{32,9... | collective-permute-start | bytes 1572872 | tf_op jit(solution)/shard_map/ppermute | solution.py:19
  462.4 34.9 %collective-permute-start.18 = (bf16[512,4,128]{2,0,1:T(8,128)(2,1)}, bf16[512,4,128]{2,0,1:T(8,128)(2,1)}, u32[]{:S(2)}, u32[]{:S(2)}) collective-permute-start(bf16[512,4,128]{2,0,1:T(8,128)(2,1)} %get-tuple-element.40), channel_id=1, source_target_pairs={{0,64},{4,68},{8,72},{12,76},{16,80},{20,84},{24,88},{28,92},{32,9... | collective-permute-start | bytes 1572872 | tf_op jit(solution)/shard_map/ppermute | solution.py:19
  474.0 40.5 %collective-permute-start.35 = (bf16[512,4,128]{2,0,1:T(8,128)(2,1)}, bf16[512,4,128]{2,0,1:T(8,128)(2,1)}, u32[]{:S(2)}, u32[]{:S(2)}) collective-permute-start(bf16[512,4,128]{2,0,1:T(8,128)(2,1)} %get-tuple-element.34), channel_id=1, source_target_pairs={{0,128},{4,132},{8,136},{12,140},{16,144},{20,148},{24,152},{28,15... | collective-permute-start | bytes 1572872 | tf_op jit(solution)/shard_map/ppermute | solution.py:19
  479.8 30.9 %collective-permute-start.29 = (bf16[512,4,128]{2,0,1:T(8,128)(2,1)}, bf16[512,4,128]{2,0,1:T(8,128)(2,1)}, u32[]{:S(2)}, u32[]{:S(2)}) collective-permute-start(bf16[512,4,128]{2,0,1:T(8,128)(2,1)} %get-tuple-element.42), channel_id=1, source_target_pairs={{0,128},{4,132},{8,136},{12,140},{16,144},{20,148},{24,152},{28,15... | collective-permute-start | bytes 1572872 | tf_op jit(solution)/shard_map/ppermute | solution.py:19
  497.3 23.6 %collective-permute-start.49 = (bf16[512,4,128]{2,0,1:T(8,128)(2,1)}, bf16[512,4,128]{2,0,1:T(8,128)(2,1)S(1)}, u32[]{:S(2)}, u32[]{:S(2)}) collective-permute-start(bf16[512,4,128]{2,0,1:T(8,128)(2,1)} %copy-done.64), channel_id=1, source_target_pairs={{0,256},{4,260},{8,264},{12,268},{16,272},{20,276},{24,280},{28,28... | collective-permute-start | bytes 1572872 | tf_op jit(solution)/shard_map/ppermute | solution.py:19
  503.0 14.2 %collective-permute-start.42 = (bf16[512,4,128]{2,0,1:T(8,128)(2,1)}, bf16[512,4,128]{2,0,1:T(8,128)(2,1)}, u32[]{:S(2)}, u32[]{:S(2)}) collective-permute-start(bf16[512,4,128]{2,0,1:T(8,128)(2,1)} %get-tuple-element.44), channel_id=1, source_target_pairs={{0,256},{4,260},{8,264},{12,268},{16,272},{20,276},{24,280},{28,28... | collective-permute-start | bytes 1572872 | tf_op jit(solution)/shard_map/ppermute | solution.py:19
  (70 other events, 2223.9 us)
Sparse Core Ops, SparseCore 0:
  540.4 79.0 reduce-scatter.1
where the time goes:
time: 634 us; the launch traced here: 628 us
  waiting for transfers between devices  231 us (36%)
  starting transfers between devices  217 us (34%)
  local copies, waits for them, and re-layouts  98.7 us (16%)
  other arithmetic  39.6 us (6%)
  matrix products  27.1 us (4%)
  between operations  15 us (2%)
    ppermute x50, starting transfers between devices, from_partner(): return lax.ppermute(value, axis, pairs)  217 us
    ppermute x50, waiting for transfers between devices, from_partner(): return lax.ppermute(value, axis, pairs)  152 us
    reduce_scatter x1, waiting for transfers between devices, per_device(): lax.psum_scatter(jnp.dot(attention, out_weight, preferred_element_type=jn...  79.2 us
    unnamed x173, local copies, waits for them, and re-layouts  30.5 us
    broadcast_in_dim x28, local copies, waits for them, and re-layouts, spread_rows(): expanded = jnp.where(onehot[None, :, :], selected[:, None, :], fill_value)  17.7 us
    add x17, local copies, waits for them, and re-layouts, per_device(): owners[:, None, None] * rows_dev + pattern[None, :, :]  14.5 us
  transfers between devices with their start and end apart: 51, of which 10 were waited for; matrix products, arithmetic and copies ran while one was open for 23% of the time, Pallas kernels for 0%

commit v1 on v0

v1 whole, which is shorter than its diff:
```python
import functools
import math

import jax
import jax.numpy as jnp
from jax import lax
from jax.experimental import pallas as pl
from jax.experimental.pallas import tpu as pltpu
from jax.sharding import PartitionSpec as P

HEAD_DIM = 128
ROWS = 128
LOCAL_HEADS = 4
X = 4
D = 2048
COLS = D // 2
NCOL = D // COLS
NEG = -1e30
MESH = pl.DeviceIdType.MESH
F32, BF16 = jnp.float32, jnp.bfloat16
SCALE = math.log2(math.e) / math.sqrt(HEAD_DIM)


def dot(a, b):
    return lax.dot_general(a, b, (((1,), (0,)), ((), ())), preferred_element_type=F32)


def dot_t(a, b):
    return lax.dot_general(a, b, (((1,), (1,)), ((), ())), preferred_element_type=F32)


def position(r, h):
    return jnp.where(
        r < 8,
        lax.rem(h, 16) + 16 * r,
        jnp.where(
            r < 16,
            lax.rem(h + 8, 16) + 16 * (r - 8),
            jnp.where(
                r < 32,
                lax.rem(h + 4, 8) + 8 * (r - 16),
                jnp.where(r < 64, lax.rem(h + 2, 4) + 4 * (r - 32), lax.rem(h + 1, 2) + 2 * (r - 64)),
            ),
        ),
    )


def kernel(
    q_ref, k_ref, v_ref, w_hbm, o_ref,
    perm, tiny, blocks, pre, r1, r2, r3, r4, l0, stat, top, den, num, ao, att, w_ref, part, out_buf, rs,
    s_w, s_tiny, s_p3, s_p2, s_p1, s_blk, s_fwd, s_chain, s_l0, s_ret, s_rs,
    r_blk, r_pre, r_1, r_2, r_3, r_4, r_l0, r_att, r_rs,
):
    s, x = lax.axis_index("seq"), lax.axis_index("head")
    c, i, g, y = lax.rem(s, 2), lax.rem(s // 2, 4), lax.rem(s // 8, 4), s // 32
    me = 2 * i + c
    base = s - me

    def group(y_, g_):
        return y_ * 32 + g_ * 8

    y_near = y + 1 - 2 * lax.rem(y, 2)
    g_near = g + 1 - 2 * lax.rem(g, 2)
    base_g1, base_g3 = group(y, g_near), group(y, 3 - g)
    base_y1, base_y3 = group(y_near, g), group(3 - y, g)
    upper1, upper2 = lax.rem(g, 2) == 1, g >= 2
    upper3, upper4 = lax.rem(y, 2) == 1, y >= 2
    lower1, lower2, lower3, lower4 = g - 2 * (g // 2) == 0, g < 2, lax.rem(y, 2) == 0, y < 2
    core0, core1 = c == 0, c == 1

    w_copy = pltpu.make_async_copy(w_hbm, w_ref, s_w)
    w_copy.start()

    barrier = pltpu.get_barrier_semaphore()

    def greet(s_, x_):
        pl.semaphore_signal(barrier, inc=1, device_id=(s_, x_), device_id_type=MESH)

    for n in range(8):
        for there in (base_g1, base_g3, base_y1, base_y3):
            if n % 2 == 1:
                greet(there + n, x)
            else:
                pl.when(core1)(functools.partial(greet, there + n, x))
        pl.when(me != n)(functools.partial(greet, base + n, x))
    for d in range(1, X):
        greet(s, lax.rem(x + d, X))

    row = lax.broadcasted_iota(jnp.int32, (ROWS, ROWS), 0)
    lane = lax.broadcasted_iota(jnp.int32, (ROWS, ROWS), 1)
    for j in range(LOCAL_HEADS):
        cols = slice(j * HEAD_DIM, (j + 1) * HEAD_DIM)
        pick = jnp.where(lane == position(row, LOCAL_HEADS * x + j), 1.0, 0.0).astype(BF16)
        picked = [dot(pick, ref[:, cols]) for ref in (q_ref, k_ref, v_ref)]
        for n in range(3):
            perm[j, n] = picked[n].astype(BF16)
        tiny[j] = jnp.concatenate([picked[1][:8], picked[2][:8]], axis=0).astype(BF16)

    pl.semaphore_wait(barrier, 26 + 16 * c)

    sends = []

    def send(cond, src, dst, ssem, rsem, s_, x_=None):
        copy = pltpu.make_async_remote_copy(
            src_ref=src, dst_ref=dst, send_sem=ssem, recv_sem=rsem,
            device_id=(s_, x if x_ is None else x_), device_id_type=MESH,
        )
        sends.append((cond, copy))
        if cond is None:
            copy.start()
        else:
            pl.when(cond)(copy.start)

    def arrived(ref, sem):
        pltpu.make_async_copy(ref, ref, sem).wait()

    for j in range(LOCAL_HEADS):
        send(lower4, tiny.at[j], r4.at[0, me], s_tiny.at[j], r_4.at[0], base_y3 + 2 * j + 1)
    for j in range(LOCAL_HEADS):
        send(lower3, perm.at[j, 1:3, 0:16], r3.at[0, me], s_p3.at[j], r_3.at[0], base_y1 + 2 * j + 1)
    for j in range(LOCAL_HEADS):
        send(lower2, perm.at[j, 1:3, 0:32], r2.at[0, me], s_p2.at[j], r_2.at[0], base_g3 + 2 * j + 1)
    for j in range(LOCAL_HEADS):
        send(me != 2 * j, perm.at[j], blocks.at[me], s_blk.at[j], r_blk.at[me], base + 2 * j)
    for j in range(LOCAL_HEADS):
        send(lower1, perm.at[j, 1:3, 0:64], r1.at[me], s_p1.at[j], r_1, base_g1 + 2 * j + 1)

    head = LOCAL_HEADS * x + i

    def send_back(b, lo):
        there = base + b
        pl.when(me != b)(
            pltpu.make_async_remote_copy(
                src_ref=ao.at[b], dst_ref=att.at[i, lo : lo + 64], send_sem=s_ret.at[b],
                recv_sem=r_att.at[i, lo // 64], device_id=(there, x), device_id_type=MESH,
            ).start
        )

        @pl.when(me == b)
        def _():
            att[i, lo : lo + 64] = ao[b]

    def wait_back(b, lo):
        pl.when(me != b)(
            pltpu.make_async_remote_copy(
                src_ref=ao.at[b], dst_ref=att.at[i, lo : lo + 64], send_sem=s_ret.at[b],
                recv_sem=r_att.at[i, lo // 64], device_id=(base + b, x), device_id_type=MESH,
            ).wait_send
        )

    @pl.when(core0)
    def _():
        blocks[me] = perm[i]

        def forward(b):
            return pltpu.make_async_remote_copy(
                src_ref=blocks.at[b, :, 0:64], dst_ref=pre.at[b], send_sem=s_fwd.at[b], recv_sem=r_pre.at[b],
                device_id=(s + 1, x), device_id_type=MESH,
            )

        def hand(b):
            return pltpu.make_async_remote_copy(
                src_ref=stat.at[b], dst_ref=l0.at[b], send_sem=s_l0.at[b], recv_sem=r_l0.at[b],
                device_id=(s + 1, x), device_id_type=MESH,
            )

        for b in range(8):
            pl.when(me != b)(functools.partial(arrived, blocks.at[b], r_blk.at[b]))
            forward(b).start()
        same = position(lane, head) <= position(row, head)
        half = lax.broadcasted_iota(jnp.int32, (64, ROWS), 1) < 64
        for b in range(8):
            width = ROWS * (b + 1)
            keys = blocks[0 : b + 1, 1].reshape(width, HEAD_DIM)
            values = blocks[0 : b + 1, 2].reshape(width, HEAD_DIM)
            scores = dot_t(blocks[b, 0], keys) * SCALE
            last = jnp.where(same, scores[:, ROWS * b :], NEG)
            scores = last if b == 0 else jnp.concatenate([scores[:, : ROWS * b], last], axis=1)
            peak = jnp.max(scores, axis=1, keepdims=True)
            weights = jnp.exp2(scores - peak)
            total = jnp.sum(weights, axis=1, keepdims=True)
            numer = dot(weights.astype(BF16), values)
            stat[b, 0] = numer[:64]
            stat[b, 1] = jnp.where(half, peak[:64], total[:64])
            hand(b).start()
            ao[b] = (numer[64:] / total[64:]).astype(BF16)
            send_back(b, 64)
        for b in range(8):
            forward(b).wait_send()
            hand(b).wait_send()
            wait_back(b, 64)

    @pl.when(core1)
    def _():
        twin1, twin3 = base_g1 + me, base_g3 + me
        twin_y1 = base_y1 + me

        def chain(n, src, dst, rsem, there):
            return pltpu.make_async_remote_copy(
                src_ref=src, dst_ref=dst, send_sem=s_chain.at[n], recv_sem=rsem,
                device_id=(there, x), device_id_type=MESH,
            )

        c4a = chain(0, r4.at[0], r4.at[1], r_4.at[1], twin_y1)
        c4b = chain(1, r4.at[0:2], r4.at[2:4], r_4.at[2], twin1)
        c4c = chain(2, r4.at[0:4], r4.at[4:8], r_4.at[3], twin3)
        c3a = chain(3, r3.at[0], r3.at[1], r_3.at[1], twin1)
        c3b = chain(4, r3.at[0:2], r3.at[2:4], r_3.at[2], twin3)
        c2a = chain(5, r2.at[0], r2.at[1], r_2.at[1], twin1)

        @pl.when(upper4)
        def _():
            arrived(r4.at[0], r_4.at[0])
            c4a.start()

        @pl.when(upper3)
        def _():
            arrived(r3.at[0], r_3.at[0])
            c3a.start()

        @pl.when(upper2)
        def _():
            arrived(r2.at[0], r_2.at[0])
            c2a.start()

        @pl.when(upper4)
        def _():
            arrived(r4.at[1], r_4.at[1])
            c4b.start()

        @pl.when(upper3)
        def _():
            arrived(r3.at[1], r_3.at[1])
            c3b.start()

        @pl.when(upper4)
        def _():
            arrived(r4.at[2:4], r_4.at[2])
            c4c.start()

        for b in range(8):
            arrived(pre.at[b], r_pre.at[b])

        def update(w, keys, values, mask=None, first=False, roll=False):
            nb = ROWS // w
            for b0 in range(0, 8, nb):
                at = (slice(b0, b0 + nb), slice(0, w))
                query = pre[b0 : b0 + nb, 0, 0:w].reshape(ROWS, HEAD_DIM)
                scores = dot_t(query, keys) * SCALE
                if mask is not None:
                    scores = jnp.where(mask(b0 * w, scores.shape), scores, NEG)
                peak = jnp.max(scores, axis=1, keepdims=True)
                if first:
                    peak = jnp.broadcast_to(peak, (ROWS, HEAD_DIM))
                else:
                    was = top[at].reshape(ROWS, HEAD_DIM)
                    peak = jnp.maximum(was, peak)
                    keep = jnp.exp2(was - peak)
                weights = jnp.exp2(scores - peak[:, :1])
                total = jnp.sum(weights, axis=1, keepdims=True)
                if roll:
                    weights = pltpu.roll(weights, 8, axis=1)
                numer = dot(weights.astype(BF16), values)
                if first:
                    total = jnp.broadcast_to(total, (ROWS, HEAD_DIM))
                else:
                    total = total + den[at].reshape(ROWS, HEAD_DIM) * keep
                    numer = numer + num[at].reshape(ROWS, HEAD_DIM) * keep
                top[at] = peak.reshape(nb, w, HEAD_DIM)
                den[at] = total.reshape(nb, w, HEAD_DIM)
                num[at] = numer.reshape(nb, w, HEAD_DIM)

        def place(n, w):
            return n // w * ROWS + position(lax.rem(n, w), head)

        def causal(w, start, shape):
            query = start + lax.broadcasted_iota(jnp.int32, shape, 0)
            key = lax.broadcasted_iota(jnp.int32, shape, 1)
            return place(key, w) <= place(query, w)

        def thin(start, shape):
            query = lax.broadcasted_iota(jnp.int32, shape, 0)
            key = lax.broadcasted_iota(jnp.int32, shape, 1)
            return (lax.rem(query, 16) < 8) & (lax.rem(key, 16) < 8)

        def thin_causal(start, shape):
            return thin(start, shape) & causal(16, start, shape)

        def own(n, w):
            return pre[:, n, 0:w].reshape(8 * w, HEAD_DIM)

        update(64, own(1, 64), own(2, 64), functools.partial(causal, 64), first=True)
        update(32, own(1, 32), own(2, 32), functools.partial(causal, 32))
        update(16, own(1, 16), own(2, 16), functools.partial(causal, 16))
        update(16, own(1, 16), own(2, 16), thin_causal)

        def level_rows(ref, n, w, rows):
            return ref[..., n, 0:w, :].reshape(rows, HEAD_DIM)

        @pl.when(upper2)
        def _():
            arrived(r2.at[1], r_2.at[1])
            update(32, level_rows(r2, 0, 32, 512), level_rows(r2, 1, 32, 512))
            keys, values = level_rows(r2, 0, 16, 256), level_rows(r2, 1, 16, 256)
            update(16, keys, values)
            update(16, keys, values, thin)

        @pl.when(upper3)
        def _():
            arrived(r3.at[2:4], r_3.at[2])
            keys, values = level_rows(r3, 0, 16, 512), level_rows(r3, 1, 16, 512)
            update(16, keys, values)
            update(16, keys, values, thin)

        @pl.when(upper4)
        def _():
            arrived(r4.at[4:8], r_4.at[3])
            both = r4[...].reshape(1024, HEAD_DIM)
            update(16, both, both, thin, roll=True)

        @pl.when(upper1)
        def _():
            arrived(r1, r_1)
            update(64, level_rows(r1, 0, 64, 512), level_rows(r1, 1, 64, 512))
            update(32, level_rows(r1, 0, 32, 256), level_rows(r1, 1, 32, 256))
            keys, values = level_rows(r1, 0, 16, 128), level_rows(r1, 1, 16, 128)
            update(16, keys, values)
            update(16, keys, values, thin)

        for b in range(8):
            arrived(l0.at[b], r_l0.at[b])
            peak, total = l0[b, 1, :, 0:1], l0[b, 1, :, 64:65]
            was = top[b]
            best = jnp.maximum(was, peak)
            keep, gain = jnp.exp2(was - best), jnp.exp2(peak - best)
            numer = num[b] * keep + l0[b, 0] * gain
            total = den[b] * keep + total * gain
            ao[b] = (numer / total).astype(BF16)
            send_back(b, 0)
        for b in range(8):
            wait_back(b, 0)

        @pl.when(upper4)
        def _():
            c4a.wait_send()
            c4b.wait_send()
            c4c.wait_send()

        @pl.when(upper3)
        def _():
            c3a.wait_send()
            c3b.wait_send()

        @pl.when(upper2)
        def _():
            c2a.wait_send()

    w_copy.wait()
    heads = []
    for j in range(LOCAL_HEADS):
        for half in range(2):
            sender = 2 * j + (1 - half)
            pl.when(me != sender)(
                functools.partial(arrived, att.at[j, 64 * half : 64 * half + 64], r_att.at[j, half])
            )
        pick = jnp.where(row == position(lane, LOCAL_HEADS * x + j), 1.0, 0.0).astype(BF16)
        heads.append(dot(pick, att[j]).astype(BF16))
    attention = jnp.concatenate(heads, axis=1)
    for n in range(NCOL):
        cols = slice(n * COLS, (n + 1) * COLS)
        product = dot(attention, w_ref[:, cols])
        part[n] = product
        out_buf[n] = product.astype(BF16)
        for d in range(1, X):
            there = lax.rem(x + d, X)
            send(
                None, out_buf.at[n, pl.ds(pl.multiple_of(32 * there, 32), 32)], rs.at[n, d - 1],
                s_rs.at[n, d - 1], r_rs.at[n, d - 1], s, there,
            )
    for n in range(NCOL):
        total = part[n, pl.ds(pl.multiple_of(32 * x, 32), 32)]
        for d in range(1, X):
            arrived(rs.at[n, d - 1], r_rs.at[n, d - 1])
            total = total + rs[n, d - 1].astype(F32)
        o_ref[:, n * COLS : (n + 1) * COLS] = total.astype(BF16)
    for cond, copy in sends:
        if cond is None:
            copy.wait_send()
        else:
            pl.when(cond)(copy.wait_send)


def per_device(query_rows, key_rows, value_rows, out_weight):
    vmem = pl.BlockSpec(memory_space=pltpu.VMEM)
    dma = pltpu.SemaphoreType.DMA
    hd = HEAD_DIM
    return pl.pallas_call(
        kernel,
        out_shape=jax.ShapeDtypeStruct((ROWS // X, D), BF16),
        in_specs=[vmem, vmem, vmem, pl.BlockSpec(memory_space=pl.ANY)],
        out_specs=vmem,
        scratch_shapes=[
            pltpu.VMEM((LOCAL_HEADS, 3, ROWS, hd), BF16),
            pltpu.VMEM((LOCAL_HEADS, 16, hd), BF16),
            pltpu.VMEM((8, 3, ROWS, hd), BF16),
            pltpu.VMEM((8, 3, 64, hd), BF16),
            pltpu.VMEM((8, 2, 64, hd), BF16),
            pltpu.VMEM((2, 8, 2, 32, hd), BF16),
            pltpu.VMEM((4, 8, 2, 16, hd), BF16),
            pltpu.VMEM((8, 8, 16, hd), BF16),
            pltpu.VMEM((8, 2, 64, hd), F32),
            pltpu.VMEM((8, 2, 64, hd), F32),
            pltpu.VMEM((8, 64, hd), F32),
            pltpu.VMEM((8, 64, hd), F32),
            pltpu.VMEM((8, 64, hd), F32),
            pltpu.VMEM((8, 64, hd), BF16),
            pltpu.VMEM((LOCAL_HEADS, ROWS, hd), BF16),
            pltpu.VMEM((LOCAL_HEADS * hd, D), BF16),
            pltpu.VMEM((NCOL, ROWS, COLS), F32),
            pltpu.VMEM((NCOL, ROWS, COLS), BF16),
            pltpu.VMEM((NCOL, X - 1, ROWS // X, COLS), BF16),
            dma, dma((4,)), dma((4,)), dma((4,)), dma((4,)), dma((4,)), dma((8,)), dma((6,)),
            dma((8,)), dma((8,)), dma((NCOL, X - 1)),
            dma((8,)), dma((8,)), dma, dma((2,)), dma((3,)), dma((4,)), dma((8,)), dma((4, 2)),
            dma((NCOL, X - 1)),
        ],
        compiler_params=pltpu.CompilerParams(
            collective_id=0, has_side_effects=True, vmem_limit_bytes=48 * 1024 * 1024
        ),
    )(query_rows, key_rows, value_rows, out_weight)


def solution(mesh):
    in_specs = (P("seq", "head"), P("seq", "head"), P("seq", "head"), P("head", None))
    return jax.shard_map(
        per_device, mesh=mesh, in_specs=in_specs, out_specs=P(("seq", "head"), None), check_vma=False
    )
```

time: 634 us -> 71.1 us (0.11)
  the two profiles are of different devices: /device:TPU:17 before, /device:TPU:24 now
where the time goes in v1:
time: 71.1 us; the launch traced here: 70.9 us
  Pallas kernels  65.9 us (93%)
  local copies, waits for them, and re-layouts  4.96 us (7%)
    pallas_call x1, Pallas kernels, per_device(): pl.pallas_call(kernel, out_shape=jax.ShapeDtypeStruct((ROWS // X, D), BF1...  65.9 us
    unnamed x9, local copies, waits for them, and re-layouts  4.96 us

profile of v1, /device:TPU:24, one launch (start us, length us, event | category | flops | bytes accessed | tf_op | source)
XLA Modules:
  0.0 70.9 jit_solution(4815930655111857471)
XLA Ops:
  0.0 0.0 copy-start
  0.0 1.6 %copy-done = bf16[512,2048]{1,0:T(8,128)(2,1)S(1)} copy-done((bf16[512,2048]{1,0:T(8,128)(2,1)S(1)}, bf16[512,2048]{1,0:T(8,128)(2,1)}, u32[]{:S(2)}) %copy-start) | copy-done | bytes 2097176
  1.6 0.0 copy-start.1
  1.6 0.9 %copy-done.1 = bf16[128,512]{1,0:T(8,128)(2,1)S(1)} copy-done((bf16[128,512]{1,0:T(8,128)(2,1)S(1)}, bf16[128,512]{1,0:T(8,128)(2,1)}, u32[]{:S(2)}) %copy-start.1) | copy-done | bytes 131096
  2.5 0.0 copy-start.2
  2.5 0.9 %copy-done.2 = bf16[128,512]{1,0:T(8,128)(2,1)S(1)} copy-done((bf16[128,512]{1,0:T(8,128)(2,1)S(1)}, bf16[128,512]{1,0:T(8,128)(2,1)}, u32[]{:S(2)}) %copy-start.2) | copy-done | bytes 131096
  3.4 0.0 copy-start.3
  3.4 0.9 %copy-done.3 = bf16[128,512]{1,0:T(8,128)(2,1)S(1)} copy-done((bf16[128,512]{1,0:T(8,128)(2,1)S(1)}, bf16[128,512]{1,0:T(8,128)(2,1)}, u32[]{:S(2)}) %copy-start.3) | copy-done | bytes 131096
  4.3 65.9 %shard_map.46 = bf16[32,2048]{1,0:T(8,128)(2,1)S(1)} custom-call(bf16[128,512]{1,0:T(8,128)(2,1)S(1)} %copy-done.1, bf16[128,512]{1,0:T(8,128)(2,1)S(1)} %copy-done.2, bf16[128,512]{1,0:T(8,128)(2,1)S(1)} %copy-done.3, bf16[512,2048]{1,0:T(8,128)(2,1)S(1)} %copy-done), custom_call_target="tpu_custom_call" | custom-call | tf_op jit(solution)/shard_map/pallas_call | solution.py:397
  70.2 0.7 copy.6
Async XLA Ops:
  0.0 1.6 %copy-start = (bf16[512,2048]{1,0:T(8,128)(2,1)S(1)}, bf16[512,2048]{1,0:T(8,128)(2,1)}, u32[]{:S(2)}) copy-start(bf16[512,2048]{1,0:T(8,128)(2,1)} %w_hbm.1) | copy-start | bytes 6291460
  1.6 0.9 %copy-start.1 = (bf16[128,512]{1,0:T(8,128)(2,1)S(1)}, bf16[128,512]{1,0:T(8,128)(2,1)}, u32[]{:S(2)}) copy-start(bf16[128,512]{1,0:T(8,128)(2,1)} %q_ref.1) | copy-start | bytes 393220
  2.5 0.9 %copy-start.2 = (bf16[128,512]{1,0:T(8,128)(2,1)S(1)}, bf16[128,512]{1,0:T(8,128)(2,1)}, u32[]{:S(2)}) copy-start(bf16[128,512]{1,0:T(8,128)(2,1)} %k_ref.1) | copy-start | bytes 393220
  3.4 0.9 %copy-start.3 = (bf16[128,512]{1,0:T(8,128)(2,1)S(1)}, bf16[128,512]{1,0:T(8,128)(2,1)}, u32[]{:S(2)}) copy-start(bf16[128,512]{1,0:T(8,128)(2,1)} %v_ref.1) | copy-start | bytes 393220

commit v2 on v1

--- a/solution.py
+++ b/solution.py
@@ -46,28 +46,27 @@
 
 
 def kernel(
-    q_ref, k_ref, v_ref, w_hbm, o_ref,
-    perm, tiny, blocks, pre, r1, r2, r3, r4, l0, stat, top, den, num, ao, att, w_ref, part, out_buf, rs,
-    s_w, s_tiny, s_p3, s_p2, s_p1, s_blk, s_fwd, s_chain, s_l0, s_ret, s_rs,
-    r_blk, r_pre, r_1, r_2, r_3, r_4, r_l0, r_att, r_rs,
+    q_hbm, k_hbm, v_hbm, w_hbm, o_ref,
+    q_ref, k_ref, v_ref, perm, blocks, pre, r1, r2, rv, ry, l0, stat, top, den, num, ao, att, w_ref, part, out_buf, rs,
+    go, s_in, s_w, s_p1, s_p2, s_pv, s_blk, s_fwd, s_y, s_l0, s_ret, s_rs,
+    r_blk, r_pre, r_1, r_2, r_v, r_y, r_l0, r_att, r_rs,
 ):
     s, x = lax.axis_index("seq"), lax.axis_index("head")
     c, i, g, y = lax.rem(s, 2), lax.rem(s // 2, 4), lax.rem(s // 8, 4), s // 32
     me = 2 * i + c
     base = s - me
 
-    def group(y_, g_):
-        return y_ * 32 + g_ * 8
-
-    y_near = y + 1 - 2 * lax.rem(y, 2)
-    g_near = g + 1 - 2 * lax.rem(g, 2)
-    base_g1, base_g3 = group(y, g_near), group(y, 3 - g)
-    base_y1, base_y3 = group(y_near, g), group(3 - y, g)
+    line = y * 32
     upper1, upper2 = lax.rem(g, 2) == 1, g >= 2
-    upper3, upper4 = lax.rem(y, 2) == 1, y >= 2
-    lower1, lower2, lower3, lower4 = g - 2 * (g // 2) == 0, g < 2, lax.rem(y, 2) == 0, y < 2
+    lower1, lower2 = lax.rem(g, 2) == 0, g < 2
     core0, core1 = c == 0, c == 1
 
+    loads = [
+        pltpu.make_async_copy(src, dst, s_in.at[n])
+        for n, (src, dst) in enumerate(((q_hbm, q_ref), (k_hbm, k_ref), (v_hbm, v_ref)))
+    ]
+    for load in loads:
+        load.start()
     w_copy = pltpu.make_async_copy(w_hbm, w_ref, s_w)
     w_copy.start()
 
@@ -76,27 +75,43 @@
     def greet(s_, x_):
         pl.semaphore_signal(barrier, inc=1, device_id=(s_, x_), device_id_type=MESH)
 
-    for n in range(8):
-        for there in (base_g1, base_g3, base_y1, base_y3):
-            if n % 2 == 1:
-                greet(there + n, x)
-            else:
-                pl.when(core1)(functools.partial(greet, there + n, x))
-        pl.when(me != n)(functools.partial(greet, base + n, x))
+    @pl.when(core0)
+    def _():
+        for n in range(0, 8, 2):
+            pl.when(me != n)(functools.partial(greet, base + n, x))
+
+    @pl.when(core1)
+    def _():
+        for n in range(0, 8, 2):
+            greet(base + n, x)
+        for d in range(1, 4):
+            for n in range(1, 8, 2):
+                greet(line + 8 * lax.rem(g + d, 4) + n, x)
+            greet(lax.rem(s + 32 * d, 128), x)
+
     for d in range(1, X):
         greet(s, lax.rem(x + d, X))
 
+    for load in loads:
+        load.wait()
     row = lax.broadcasted_iota(jnp.int32, (ROWS, ROWS), 0)
     lane = lax.broadcasted_iota(jnp.int32, (ROWS, ROWS), 1)
     for j in range(LOCAL_HEADS):
         cols = slice(j * HEAD_DIM, (j + 1) * HEAD_DIM)
         pick = jnp.where(lane == position(row, LOCAL_HEADS * x + j), 1.0, 0.0).astype(BF16)
-        picked = [dot(pick, ref[:, cols]) for ref in (q_ref, k_ref, v_ref)]
-        for n in range(3):
-            perm[j, n] = picked[n].astype(BF16)
-        tiny[j] = jnp.concatenate([picked[1][:8], picked[2][:8]], axis=0).astype(BF16)
-
-    pl.semaphore_wait(barrier, 26 + 16 * c)
+        for n, ref in enumerate((q_ref, k_ref, v_ref)):
+            perm[j, n] = dot(pick, ref[:, cols]).astype(BF16)
+
+    @pl.when(core0)
+    def _():
+        pl.semaphore_wait(barrier, 10)
+        for n in range(1, 8, 2):
+            pl.semaphore_signal(go, inc=1, device_id=(base + n, x), device_id_type=MESH)
+
+    @pl.when(core1)
+    def _():
+        pl.semaphore_wait(go, 4)
+
 
     sends = []
 
@@ -114,16 +129,41 @@
     def arrived(ref, sem):
         pltpu.make_async_copy(ref, ref, sem).wait()
 
+    def regroup(cond):
+        for j in range(LOCAL_HEADS):
+            send(
+                cond & (me != 2 * j), perm.at[j], blocks.at[me], s_blk.at[j], r_blk.at[me], base + 2 * j
+            )
+
+    regroup(g < 2)
+
+    @pl.when(core1)
+    def _():
+        pl.semaphore_wait(barrier, 18)
+        pl.semaphore_signal(go, inc=1, device_id=(s - 1, x), device_id_type=MESH)
+
+    @pl.when(core0)
+    def _():
+        pl.semaphore_wait(go, 1)
+
+    for h in range(4):
+        for j in range(LOCAL_HEADS):
+            cond = (y < 3) & (g >= h) & ((g != h) | (me != 2 * j + 1))
+            send(cond, perm.at[j, 1:3, 0:16], rv.at[g, me], s_pv.at[h, j], r_v.at[g], line + 8 * h + 2 * j + 1)
+
+    @pl.when((y < 3) & core1)
+    def _():
+        rv[g, me] = perm[i, 1:3, 0:16]
+
+    for h in range(2):
+        for j in range(LOCAL_HEADS):
+            send(
+                lower2, perm.at[j, 1:3, 0:32], r2.at[g, me], s_p2.at[h, j], r_2.at[g],
+                line + 8 * (2 + h) + 2 * j + 1,
+            )
     for j in range(LOCAL_HEADS):
-        send(lower4, tiny.at[j], r4.at[0, me], s_tiny.at[j], r_4.at[0], base_y3 + 2 * j + 1)
-    for j in range(LOCAL_HEADS):
-        send(lower3, perm.at[j, 1:3, 0:16], r3.at[0, me], s_p3.at[j], r_3.at[0], base_y1 + 2 * j + 1)
-    for j in range(LOCAL_HEADS):
-        send(lower2, perm.at[j, 1:3, 0:32], r2.at[0, me], s_p2.at[j], r_2.at[0], base_g3 + 2 * j + 1)
-    for j in range(LOCAL_HEADS):
-        send(me != 2 * j, perm.at[j], blocks.at[me], s_blk.at[j], r_blk.at[me], base + 2 * j)
-    for j in range(LOCAL_HEADS):
-        send(lower1, perm.at[j, 1:3, 0:64], r1.at[me], s_p1.at[j], r_1, base_g1 + 2 * j + 1)
+        send(lower1, perm.at[j, 1:3, 0:64], r1.at[me], s_p1.at[j], r_1, base + 8 + 2 * j + 1)
+    regroup(g >= 2)
 
     head = LOCAL_HEADS * x + i
 
@@ -192,56 +232,36 @@
 
     @pl.when(core1)
     def _():
-        twin1, twin3 = base_g1 + me, base_g3 + me
-        twin_y1 = base_y1 + me
-
-        def chain(n, src, dst, rsem, there):
-            return pltpu.make_async_remote_copy(
-                src_ref=src, dst_ref=dst, send_sem=s_chain.at[n], recv_sem=rsem,
-                device_id=(there, x), device_id_type=MESH,
-            )
-
-        c4a = chain(0, r4.at[0], r4.at[1], r_4.at[1], twin_y1)
-        c4b = chain(1, r4.at[0:2], r4.at[2:4], r_4.at[2], twin1)
-        c4c = chain(2, r4.at[0:4], r4.at[4:8], r_4.at[3], twin3)
-        c3a = chain(3, r3.at[0], r3.at[1], r_3.at[1], twin1)
-        c3b = chain(4, r3.at[0:2], r3.at[2:4], r_3.at[2], twin3)
-        c2a = chain(5, r2.at[0], r2.at[1], r_2.at[1], twin1)
-
-        @pl.when(upper4)
-        def _():
-            arrived(r4.at[0], r_4.at[0])
-            c4a.start()
-
-        @pl.when(upper3)
-        def _():
-            arrived(r3.at[0], r_3.at[0])
-            c3a.start()
-
-        @pl.when(upper2)
-        def _():
-            arrived(r2.at[0], r_2.at[0])
-            c2a.start()
-
-        @pl.when(upper4)
-        def _():
-            arrived(r4.at[1], r_4.at[1])
-            c4b.start()
-
-        @pl.when(upper3)
-        def _():
-            arrived(r3.at[1], r_3.at[1])
-            c3b.start()
-
-        @pl.when(upper4)
-        def _():
-            arrived(r4.at[2:4], r_4.at[2])
-            c4c.start()
+        def arrived_if(cond, ref, sem):
+            pl.when(cond)(functools.partial(arrived, ref, sem))
+
+        passes = []
+
+        def pass_on(cond, h, src):
+            for d in range(1, 4):
+                copy = pltpu.make_async_remote_copy(
+                    src_ref=src, dst_ref=ry.at[y, h], send_sem=s_y.at[d - 1, h], recv_sem=r_y.at[y],
+                    device_id=(s + 32 * d, x), device_id_type=MESH,
+                )
+                pl.when(cond & (y + d < 4))(copy.start)
+                passes.append((cond & (y + d < 4), copy))
+
+        for h in range(4):
+            later = (y < 3) & (g <= h)
+            arrived_if(later & (g != h), rv.at[h], r_v.at[h])
+            arrived_if(later & (g == h), rv.at[h, 0:7], r_v.at[h])
+            pass_on(later, h, rv.at[h])
+        for h in range(2):
+            arrived_if(upper2, r2.at[h], r_2.at[h])
+            pass_on(upper2, h, r2.at[h, :, :, 0:16])
+        arrived_if(upper1, r1, r_1)
+        for h in (0, 2):
+            pass_on(g == h + 1, h, r1.at[:, :, 0:16])
 
         for b in range(8):
             arrived(pre.at[b], r_pre.at[b])
 
-        def update(w, keys, values, mask=None, first=False, roll=False):
+        def update(w, keys, values, mask=None, first=False):
             nb = ROWS // w
             for b0 in range(0, 8, nb):
                 at = (slice(b0, b0 + nb), slice(0, w))
@@ -258,8 +278,6 @@
                     keep = jnp.exp2(was - peak)
                 weights = jnp.exp2(scores - peak[:, :1])
                 total = jnp.sum(weights, axis=1, keepdims=True)
-                if roll:
-                    weights = pltpu.roll(weights, 8, axis=1)
                 numer = dot(weights.astype(BF16), values)
                 if first:
                     total = jnp.broadcast_to(total, (ROWS, HEAD_DIM))
@@ -297,35 +315,31 @@
         def level_rows(ref, n, w, rows):
             return ref[..., n, 0:w, :].reshape(rows, HEAD_DIM)
 
-        @pl.when(upper2)
-        def _():
-            arrived(r2.at[1], r_2.at[1])
-            update(32, level_rows(r2, 0, 32, 512), level_rows(r2, 1, 32, 512))
-            keys, values = level_rows(r2, 0, 16, 256), level_rows(r2, 1, 16, 256)
-            update(16, keys, values)
-            update(16, keys, values, thin)
-
-        @pl.when(upper3)
-        def _():
-            arrived(r3.at[2:4], r_3.at[2])
-            keys, values = level_rows(r3, 0, 16, 512), level_rows(r3, 1, 16, 512)
-            update(16, keys, values)
-            update(16, keys, values, thin)
-
-        @pl.when(upper4)
-        def _():
-            arrived(r4.at[4:8], r_4.at[3])
-            both = r4[...].reshape(1024, HEAD_DIM)
-            update(16, both, both, thin, roll=True)
-
         @pl.when(upper1)
         def _():
-            arrived(r1, r_1)
             update(64, level_rows(r1, 0, 64, 512), level_rows(r1, 1, 64, 512))
             update(32, level_rows(r1, 0, 32, 256), level_rows(r1, 1, 32, 256))
             keys, values = level_rows(r1, 0, 16, 128), level_rows(r1, 1, 16, 128)
             update(16, keys, values)
             update(16, keys, values, thin)
+
+        @pl.when(upper2)
+        def _():
+            update(32, level_rows(r2, 0, 32, 512), level_rows(r2, 1, 32, 512))
+            keys, values = level_rows(r2, 0, 16, 256), level_rows(r2, 1, 16, 256)
+            update(16, keys, values)
+            update(16, keys, values, thin)
+
+        for t in range(3):
+
+            @pl.when(y > t)
+            def _(t=t):
+                arrived(ry.at[t], r_y.at[t])
+                keys = ry[t, :, :, 0].reshape(512, HEAD_DIM)
+                values = ry[t, :, :, 1].reshape(512, HEAD_DIM)
+                if t % 2 == 0:
+                    pl.when(y == t + 1)(functools.partial(update, 16, keys, values))
+                update(16, keys, values, thin)
 
         for b in range(8):
             arrived(l0.at[b], r_l0.at[b])
@@ -340,20 +354,8 @@
         for b in range(8):
             wait_back(b, 0)
 
-        @pl.when(upper4)
-        def _():
-            c4a.wait_send()
-            c4b.wait_send()
-            c4c.wait_send()
-
-        @pl.when(upper3)
-        def _():
-            c3a.wait_send()
-            c3b.wait_send()
-
-        @pl.when(upper2)
-        def _():
-            c2a.wait_send()
+        for cond, copy in passes:
+            pl.when(cond)(copy.wait_send)
 
     w_copy.wait()
     heads = []
@@ -397,17 +399,19 @@
     return pl.pallas_call(
         kernel,
         out_shape=jax.ShapeDtypeStruct((ROWS // X, D), BF16),
-        in_specs=[vmem, vmem, vmem, pl.BlockSpec(memory_space=pl.ANY)],
+        in_specs=[pl.BlockSpec(memory_space=pl.ANY)] * 4,
         out_specs=vmem,
         scratch_shapes=[
+            pltpu.VMEM((ROWS, LOCAL_HEADS * hd), BF16),
+            pltpu.VMEM((ROWS, LOCAL_HEADS * hd), BF16),
+            pltpu.VMEM((ROWS, LOCAL_HEADS * hd), BF16),
             pltpu.VMEM((LOCAL_HEADS, 3, ROWS, hd), BF16),
-            pltpu.VMEM((LOCAL_HEADS, 16, hd), BF16),
             pltpu.VMEM((8, 3, ROWS, hd), BF16),
             pltpu.VMEM((8, 3, 64, hd), BF16),
             pltpu.VMEM((8, 2, 64, hd), BF16),
             pltpu.VMEM((2, 8, 2, 32, hd), BF16),
             pltpu.VMEM((4, 8, 2, 16, hd), BF16),
-            pltpu.VMEM((8, 8, 16, hd), BF16),
+            pltpu.VMEM((3, 4, 8, 2, 16, hd), BF16),
             pltpu.VMEM((8, 2, 64, hd), F32),
             pltpu.VMEM((8, 2, 64, hd), F32),
             pltpu.VMEM((8, 64, hd), F32),
@@ -419,13 +423,14 @@
             pltpu.VMEM((NCOL, ROWS, COLS), F32),
             pltpu.VMEM((NCOL, ROWS, COLS), BF16),
             pltpu.VMEM((NCOL, X - 1, ROWS // X, COLS), BF16),
-            dma, dma((4,)), dma((4,)), dma((4,)), dma((4,)), dma((4,)), dma((8,)), dma((6,)),
+            pltpu.SemaphoreType.REGULAR,
+            dma((3,)), dma, dma((4,)), dma((2, 4)), dma((4, 4)), dma((4,)), dma((8,)), dma((3, 4)),
             dma((8,)), dma((8,)), dma((NCOL, X - 1)),
-            dma((8,)), dma((8,)), dma, dma((2,)), dma((3,)), dma((4,)), dma((8,)), dma((4, 2)),
+            dma((8,)), dma((8,)), dma, dma((2,)), dma((4,)), dma((3,)), dma((8,)), dma((4, 2)),
             dma((NCOL, X - 1)),
         ],
         compiler_params=pltpu.CompilerParams(
-            collective_id=0, has_side_effects=True, vmem_limit_bytes=48 * 1024 * 1024
+            collective_id=0, has_side_effects=True, vmem_limit_bytes=60 * 1024 * 1024
         ),
     )(query_rows, key_rows, value_rows, out_weight)
 

time: 71.1 us -> 54.4 us (0.77)
  the two profiles are of different devices: /device:TPU:24 before, /device:TPU:504 now
where the time goes in v2:
time: 54.4 us; the launch traced here: 54.3 us
  Pallas kernels  52.7 us (97%)
  local copies, waits for them, and re-layouts  1.57 us (3%)
    pallas_call x1, Pallas kernels, per_device(): pl.pallas_call(kernel, out_shape=jax.ShapeDtypeStruct((ROWS // X, D), BF1...  52.7 us
    unnamed x1, local copies, waits for them, and re-layouts  1.57 us

profile of v2, /device:TPU:504, one launch (start us, length us, event | category | flops | bytes accessed | tf_op | source)
XLA Modules:
  0.0 54.3 jit_solution(5621319026445972322)
XLA Ops:
  0.0 52.7 %shard_map.46 = bf16[32,2048]{1,0:T(8,128)(2,1)} custom-call(bf16[128,512]{1,0:T(8,128)(2,1)} %q_hbm.1, bf16[128,512]{1,0:T(8,128)(2,1)} %k_hbm.1, bf16[128,512]{1,0:T(8,128)(2,1)} %v_hbm.1, bf16[512,2048]{1,0:T(8,128)(2,1)} %w_hbm.1), custom_call_target="tpu_custom_call" | custom-call | tf_op jit(solution)/shard_map/pallas_call | solution.py:399
  52.7 1.6 %copy.6 = bf16[32,2048]{1,0:T(8,128)(2,1)} copy(bf16[32,2048]{1,0:T(8,128)(2,1)} %shard_map.46) | data formatting | bytes 262144

commit v3 on v2

--- a/solution.py
+++ b/solution.py
@@ -13,21 +13,18 @@
 LOCAL_HEADS = 4
 X = 4
 D = 2048
-COLS = D // 2
-NCOL = D // COLS
+COLS = D // 4
+CHUNK = 128
 NEG = -1e30
 MESH = pl.DeviceIdType.MESH
 F32, BF16 = jnp.float32, jnp.bfloat16
 SCALE = math.log2(math.e) / math.sqrt(HEAD_DIM)
 
-
 def dot(a, b):
     return lax.dot_general(a, b, (((1,), (0,)), ((), ())), preferred_element_type=F32)
 
-
 def dot_t(a, b):
     return lax.dot_general(a, b, (((1,), (1,)), ((), ())), preferred_element_type=F32)
-
 
 def position(r, h):
     return jnp.where(
@@ -44,12 +41,11 @@
         ),
     )
 
-
 def kernel(
     q_hbm, k_hbm, v_hbm, w_hbm, o_ref,
-    q_ref, k_ref, v_ref, perm, blocks, pre, r1, r2, rv, ry, l0, stat, top, den, num, ao, att, w_ref, part, out_buf, rs,
-    go, s_in, s_w, s_p1, s_p2, s_pv, s_blk, s_fwd, s_y, s_l0, s_ret, s_rs,
-    r_blk, r_pre, r_1, r_2, r_v, r_y, r_l0, r_att, r_rs,
+    q_ref, k_ref, v_ref, perm, blocks, pre, r1, r2, rv, ry, rp, pack, l0, stat, top, den, num, ao, att, nat, ax, w_ref, part,
+    go, s_in, s_w, s_p1, s_p2, s_pv, s_blk, s_fwd, s_y, s_l0, s_ret, s_ax, s_wx, s_wf, s_wy, s_ws,
+    r_blk, r_pre, r_1, r_2, r_v, r_y, r_l0, r_att, r_ax, r_wx, r_wf, r_wy, r_ws,
 ):
     s, x = lax.axis_index("seq"), lax.axis_index("head")
     c, i, g, y = lax.rem(s, 2), lax.rem(s // 2, 4), lax.rem(s // 8, 4), s // 32
@@ -57,6 +53,7 @@
     base = s - me
 
     line = y * 32
+    s_up, s_down = lax.rem(s + 32, 128), lax.rem(s + 96, 128)
     upper1, upper2 = lax.rem(g, 2) == 1, g >= 2
     lower1, lower2 = lax.rem(g, 2) == 0, g < 2
     core0, core1 = c == 0, c == 1
@@ -67,7 +64,7 @@
     ]
     for load in loads:
         load.start()
-    w_copy = pltpu.make_async_copy(w_hbm, w_ref, s_w)
+    w_copy = pltpu.make_async_copy(w_hbm, w_ref.at[x], s_w)
     w_copy.start()
 
     barrier = pltpu.get_barrier_semaphore()
@@ -79,6 +76,8 @@
     def _():
         for n in range(0, 8, 2):
             pl.when(me != n)(functools.partial(greet, base + n, x))
+        greet(s_up, x)
+        greet(s_down, x)
 
     @pl.when(core1)
     def _():
@@ -104,14 +103,13 @@
 
     @pl.when(core0)
     def _():
-        pl.semaphore_wait(barrier, 10)
+        pl.semaphore_wait(barrier, 12)
         for n in range(1, 8, 2):
             pl.semaphore_signal(go, inc=1, device_id=(base + n, x), device_id_type=MESH)
 
     @pl.when(core1)
     def _():
         pl.semaphore_wait(go, 4)
-
 
     sends = []
 
@@ -130,12 +128,59 @@
         pltpu.make_async_copy(ref, ref, sem).wait()
 
     def regroup(cond):
-        for j in range(LOCAL_HEADS):
-            send(
-                cond & (me != 2 * j), perm.at[j], blocks.at[me], s_blk.at[j], r_blk.at[me], base + 2 * j
-            )
+        for n in range(2):
+            part_rows = slice(64 * n, 64 * n + 64)
+            for j in range(LOCAL_HEADS):
+                send(
+                    cond & (me != 2 * j), perm.at[j, :, part_rows], blocks.at[me, :, part_rows],
+                    s_blk.at[n, j], r_blk.at[n, me], base + 2 * j,
+                )
 
     regroup(g < 2)
+
+    x_left, x_right, x_far = lax.rem(x + 3, X), lax.rem(x + 1, X), lax.rem(x + 2, X)
+    around = (x_left, x_right, x_far)
+    mine = 2 * lax.rem(y, 2)
+    theirs = 2 - mine
+    w_copy.wait()
+
+    def weight(x_, k):
+        return w_ref.at[x_, pl.ds(pl.multiple_of(k * CHUNK, CHUNK), CHUNK)]
+
+    def weight_copy(x_, k, s_, to, ssem, rsem):
+        return pltpu.make_async_remote_copy(
+            src_ref=weight(x_, k), dst_ref=weight(x_, k), send_sem=ssem, recv_sem=rsem,
+            device_id=(s_, to), device_id_type=MESH,
+        )
+
+    def own_copy(m, side):
+        to = (x_right, x_left)[side]
+        return weight_copy(x, mine + m, s, to, s_wx.at[side, m], r_wx.at[side, m])
+
+    def far_copy(m):
+        to = (x_right, x_left)[m]
+        return weight_copy(around[m], mine + m, s, to, s_wf.at[m], r_wf.at[m])
+
+    def line_copy(n, m):
+        to = (s_up, s_down)[m]
+        return weight_copy(around[n], mine + m, to, x, s_wy.at[n, m], r_wy.at[n, m])
+
+    def share_mine(n, m):
+        return weight_copy(around[n], mine + m, s + 1, x, s_ws.at[n, m], r_ws.at[n])
+
+    def share_theirs(n, m):
+        return weight_copy(around[n], theirs + m, s + 1, x, s_ws.at[n, 2 + m], r_ws.at[n])
+
+    def take_theirs(n):
+        for m in range(2):
+            arrived(weight(around[n], theirs + m), r_wy.at[n, m])
+            share_theirs(n, m).start()
+
+    @pl.when(core0)
+    def _():
+        for m in range(2):
+            own_copy(m, 0).start()
+            own_copy(1 - m, 1).start()
 
     @pl.when(core1)
     def _():
@@ -204,9 +249,24 @@
                 device_id=(s + 1, x), device_id_type=MESH,
             )
 
-        for b in range(8):
-            pl.when(me != b)(functools.partial(arrived, blocks.at[b], r_blk.at[b]))
+        for side in range(2):
+            m = side
+            arrived(weight(around[side], mine + m), r_wx.at[side, m])
+            far_copy(m).start()
+            line_copy(side, m).start()
+            share_mine(side, m).start()
+
+        for b in range(8):
+            pl.when(me != b)(functools.partial(arrived, blocks.at[b, :, 0:64], r_blk.at[0, b]))
             forward(b).start()
+        for side in range(2):
+            m = 1 - side
+            arrived(weight(around[side], mine + m), r_wx.at[side, m])
+            line_copy(side, m).start()
+            share_mine(side, m).start()
+
+        for b in range(8):
+            pl.when(me != b)(functools.partial(arrived, blocks.at[b, :, 64:128], r_blk.at[1, b]))
         same = position(lane, head) <= position(row, head)
         half = lax.broadcasted_iota(jnp.int32, (64, ROWS), 1) < 64
         for b in range(8):
@@ -225,6 +285,13 @@
             hand(b).start()
             ao[b] = (numer[64:] / total[64:]).astype(BF16)
             send_back(b, 64)
+        for m in range(2):
+            arrived(weight(x_far, mine + m), r_wf.at[m])
+            line_copy(2, m).start()
+            share_mine(2, m).start()
+        take_theirs(0)
+        take_theirs(1)
+
         for b in range(8):
             forward(b).wait_send()
             hand(b).wait_send()
@@ -238,13 +305,25 @@
         passes = []
 
         def pass_on(cond, h, src):
-            for d in range(1, 4):
+            def to_line(where, d, src, dst, rsem):
                 copy = pltpu.make_async_remote_copy(
-                    src_ref=src, dst_ref=ry.at[y, h], send_sem=s_y.at[d - 1, h], recv_sem=r_y.at[y],
+                    src_ref=src, dst_ref=dst, send_sem=s_y.at[d - 1, h], recv_sem=rsem,
                     device_id=(s + 32 * d, x), device_id_type=MESH,
                 )
-                pl.when(cond & (y + d < 4))(copy.start)
-                passes.append((cond & (y + d < 4), copy))
+                pl.when(cond & where)(copy.start)
+                passes.append((cond & where, copy))
+
+            to_line(lax.rem(y, 2) == 0, 1, src, ry.at[h], r_y.at[2])
+
+            @pl.when(cond & (y < 2))
+            def _():
+                rows = src[...].astype(F32)
+                pack[h] = jnp.concatenate([rows[:, 0, 0:8], rows[:, 1, 0:8]], axis=1).astype(BF16)
+
+            to_line(y == 0, 3, pack.at[h], rp.at[0, h], r_y.at[0])
+            to_line(y == 0, 2, pack.at[h], rp.at[0, h], r_y.at[0])
+            to_line(y == 1, 1, pack.at[h], rp.at[1, h], r_y.at[1])
+            to_line(y == 1, 2, pack.at[h], rp.at[1, h], r_y.at[1])
 
         for h in range(4):
             later = (y < 3) & (g <= h)
@@ -261,7 +340,7 @@
         for b in range(8):
             arrived(pre.at[b], r_pre.at[b])
 
-        def update(w, keys, values, mask=None, first=False):
+        def update(w, keys, values, mask=None, first=False, roll=False):
             nb = ROWS // w
             for b0 in range(0, 8, nb):
                 at = (slice(b0, b0 + nb), slice(0, w))
@@ -278,6 +357,8 @@
                     keep = jnp.exp2(was - peak)
                 weights = jnp.exp2(scores - peak[:, :1])
                 total = jnp.sum(weights, axis=1, keepdims=True)
+                if roll:
+                    weights = pltpu.roll(weights, 8, axis=1)
                 numer = dot(weights.astype(BF16), values)
                 if first:
                     total = jnp.broadcast_to(total, (ROWS, HEAD_DIM))
@@ -330,16 +411,19 @@
             update(16, keys, values)
             update(16, keys, values, thin)
 
-        for t in range(3):
-
-            @pl.when(y > t)
-            def _(t=t):
-                arrived(ry.at[t], r_y.at[t])
-                keys = ry[t, :, :, 0].reshape(512, HEAD_DIM)
-                values = ry[t, :, :, 1].reshape(512, HEAD_DIM)
-                if t % 2 == 0:
-                    pl.when(y == t + 1)(functools.partial(update, 16, keys, values))
-                update(16, keys, values, thin)
+        @pl.when(y >= 2)
+        def _():
+            for t in range(2):
+                arrived(rp.at[t], r_y.at[t])
+            both = rp[...].reshape(1024, HEAD_DIM)
+            update(16, both, both, thin, roll=True)
+
+        @pl.when(lax.rem(y, 2) == 1)
+        def _():
+            arrived(ry, r_y.at[2])
+            keys, values = ry[:, :, 0].reshape(512, HEAD_DIM), ry[:, :, 1].reshape(512, HEAD_DIM)
+            update(16, keys, values)
+            update(16, keys, values, thin)
 
         for b in range(8):
             arrived(l0.at[b], r_l0.at[b])
@@ -357,8 +441,6 @@
         for cond, copy in passes:
             pl.when(cond)(copy.wait_send)
 
-    w_copy.wait()
-    heads = []
     for j in range(LOCAL_HEADS):
         for half in range(2):
             sender = 2 * j + (1 - half)
@@ -366,31 +448,51 @@
                 functools.partial(arrived, att.at[j, 64 * half : 64 * half + 64], r_att.at[j, half])
             )
         pick = jnp.where(row == position(lane, LOCAL_HEADS * x + j), 1.0, 0.0).astype(BF16)
-        heads.append(dot(pick, att[j]).astype(BF16))
-    attention = jnp.concatenate(heads, axis=1)
-    for n in range(NCOL):
-        cols = slice(n * COLS, (n + 1) * COLS)
-        product = dot(attention, w_ref[:, cols])
-        part[n] = product
-        out_buf[n] = product.astype(BF16)
-        for d in range(1, X):
-            there = lax.rem(x + d, X)
-            send(
-                None, out_buf.at[n, pl.ds(pl.multiple_of(32 * there, 32), 32)], rs.at[n, d - 1],
-                s_rs.at[n, d - 1], r_rs.at[n, d - 1], s, there,
-            )
-    for n in range(NCOL):
-        total = part[n, pl.ds(pl.multiple_of(32 * x, 32), 32)]
-        for d in range(1, X):
-            arrived(rs.at[n, d - 1], r_rs.at[n, d - 1])
-            total = total + rs[n, d - 1].astype(F32)
-        o_ref[:, n * COLS : (n + 1) * COLS] = total.astype(BF16)
+        nat[:, j * HEAD_DIM : (j + 1) * HEAD_DIM] = dot(pick, att[j]).astype(BF16)
+
+    def quarter(x_):
+        return pl.ds(pl.multiple_of(32 * x_, 32), 32)
+
+    for d in (2, 1, 3):
+        there = lax.rem(x + d, X)
+        send(None, nat.at[quarter(there)], ax.at[x], s_ax.at[d - 1], r_ax.at[d - 1], s, there)
+
+    pl.when(core0)(functools.partial(take_theirs, 2))
+
+    for d in (0, 1, 3, 2):
+        there = lax.rem(x + X - d, X)
+        if d == 0:
+            rows = nat[quarter(x)]
+        else:
+            arrived(ax.at[there], r_ax.at[d - 1])
+            rows = ax[there]
+            n = {1: 0, 3: 1, 2: 2}[d]
+            pl.when(core1)(functools.partial(arrived, w_ref.at[there], r_ws.at[n]))
+        for n in range(D // COLS):
+            cols = slice(n * COLS, (n + 1) * COLS)
+            product = dot(rows, w_ref[there, :, cols])
+            if d > 0:
+                product = product + part[:, cols]
+            if d == 2:
+                o_ref[:, cols] = product.astype(BF16)
+            else:
+                part[:, cols] = product
+    @pl.when(core0)
+    def _():
+        for m in range(2):
+            own_copy(m, 0).wait_send()
+            own_copy(m, 1).wait_send()
+            far_copy(m).wait_send()
+            for n in range(3):
+                line_copy(n, m).wait_send()
+                share_mine(n, m).wait_send()
+                share_theirs(n, m).wait_send()
+
     for cond, copy in sends:
         if cond is None:
             copy.wait_send()
         else:
             pl.when(cond)(copy.wait_send)
-
 
 def per_device(query_rows, key_rows, value_rows, out_weight):
     vmem = pl.BlockSpec(memory_space=pltpu.VMEM)
@@ -411,7 +513,9 @@
             pltpu.VMEM((8, 2, 64, hd), BF16),
             pltpu.VMEM((2, 8, 2, 32, hd), BF16),
             pltpu.VMEM((4, 8, 2, 16, hd), BF16),
-            pltpu.VMEM((3, 4, 8, 2, 16, hd), BF16),
+            pltpu.VMEM((4, 8, 2, 16, hd), BF16),
+            pltpu.VMEM((2, 4, 8, 16, hd), BF16),
+            pltpu.VMEM((4, 8, 16, hd), BF16),
             pltpu.VMEM((8, 2, 64, hd), F32),
             pltpu.VMEM((8, 2, 64, hd), F32),
             pltpu.VMEM((8, 64, hd), F32),
@@ -419,22 +523,21 @@
             pltpu.VMEM((8, 64, hd), F32),
             pltpu.VMEM((8, 64, hd), BF16),
             pltpu.VMEM((LOCAL_HEADS, ROWS, hd), BF16),
-            pltpu.VMEM((LOCAL_HEADS * hd, D), BF16),
-            pltpu.VMEM((NCOL, ROWS, COLS), F32),
-            pltpu.VMEM((NCOL, ROWS, COLS), BF16),
-            pltpu.VMEM((NCOL, X - 1, ROWS // X, COLS), BF16),
+            pltpu.VMEM((ROWS, LOCAL_HEADS * hd), BF16),
+            pltpu.VMEM((X, ROWS // X, LOCAL_HEADS * hd), BF16),
+            pltpu.VMEM((X, LOCAL_HEADS * hd, D), BF16),
+            pltpu.VMEM((ROWS // X, D), F32),
             pltpu.SemaphoreType.REGULAR,
-            dma((3,)), dma, dma((4,)), dma((2, 4)), dma((4, 4)), dma((4,)), dma((8,)), dma((3, 4)),
-            dma((8,)), dma((8,)), dma((NCOL, X - 1)),
-            dma((8,)), dma((8,)), dma, dma((2,)), dma((4,)), dma((3,)), dma((8,)), dma((4, 2)),
-            dma((NCOL, X - 1)),
+            dma((3,)), dma, dma((4,)), dma((2, 4)), dma((4, 4)), dma((2, 4)), dma((8,)), dma((3, 4)),
+            dma((8,)), dma((8,)), dma((X - 1,)), dma((2, 2)), dma((2,)), dma((3, 2)), dma((3, 4)),
+            dma((2, 8)), dma((8,)), dma, dma((2,)), dma((4,)), dma((3,)), dma((8,)), dma((4, 2)),
+            dma((X - 1,)), dma((2, 2)), dma((2,)), dma((3, 2)), dma((3,)),
         ],
         compiler_params=pltpu.CompilerParams(
             collective_id=0, has_side_effects=True, vmem_limit_bytes=60 * 1024 * 1024
         ),
     )(query_rows, key_rows, value_rows, out_weight)
 
-
 def solution(mesh):
     in_specs = (P("seq", "head"), P("seq", "head"), P("seq", "head"), P("head", None))
     return jax.shard_map(

time: 54.4 us -> 51.2 us (0.941)
  the two profiles are of different devices: /device:TPU:504 before, /device:TPU:488 now
where the time goes in v3:
time: 51.2 us; the launch traced here: 51 us
  Pallas kernels  49.5 us (97%)
  local copies, waits for them, and re-layouts  1.57 us (3%)
    pallas_call x1, Pallas kernels, per_device(): pl.pallas_call(kernel, out_shape=jax.ShapeDtypeStruct((ROWS // X, D), BF1...  49.5 us
    unnamed x1, local copies, waits for them, and re-layouts  1.57 us

profile of v3, /device:TPU:488, one launch (start us, length us, event | category | flops | bytes accessed | tf_op | source)
XLA Modules:
  0.0 51.0 jit_solution(13381153974369170935)
XLA Ops:
  0.0 49.5 %shard_map.46 = bf16[32,2048]{1,0:T(8,128)(2,1)} custom-call(bf16[128,512]{1,0:T(8,128)(2,1)} %q_hbm.1, bf16[128,512]{1,0:T(8,128)(2,1)} %k_hbm.1, bf16[128,512]{1,0:T(8,128)(2,1)} %v_hbm.1, bf16[512,2048]{1,0:T(8,128)(2,1)} %w_hbm.1), custom_call_target="tpu_custom_call" | custom-call | tf_op jit(solution)/shard_map/pallas_call | solution.py:501
  49.5 1.6 %copy.6 = bf16[32,2048]{1,0:T(8,128)(2,1)} copy(bf16[32,2048]{1,0:T(8,128)(2,1)} %shard_map.46) | data formatting | bytes 262144

commit v4 on v3

--- a/solution.py
+++ b/solution.py
@@ -127,8 +127,8 @@
     def arrived(ref, sem):
         pltpu.make_async_copy(ref, ref, sem).wait()
 
-    def regroup(cond):
-        for n in range(2):
+    def regroup(cond, parts):
+        for n in parts:
             part_rows = slice(64 * n, 64 * n + 64)
             for j in range(LOCAL_HEADS):
                 send(
@@ -136,7 +136,8 @@
                     s_blk.at[n, j], r_blk.at[n, me], base + 2 * j,
                 )
 
-    regroup(g < 2)
+    regroup(g < 4, (0,))
+    regroup(g < 2, (1,))
 
     x_left, x_right, x_far = lax.rem(x + 3, X), lax.rem(x + 1, X), lax.rem(x + 2, X)
     around = (x_left, x_right, x_far)
@@ -193,9 +194,13 @@
 
     for h in range(4):
         for j in range(LOCAL_HEADS):
-            cond = (y < 3) & (g >= h) & ((g != h) | (me != 2 * j + 1))
+            cond = (y < 3) & ((g >= h) | (lower1 & (g + 1 == h))) & ((g != h) | (me != 2 * j + 1))
             send(cond, perm.at[j, 1:3, 0:16], rv.at[g, me], s_pv.at[h, j], r_v.at[g], line + 8 * h + 2 * j + 1)
 
+    rv_sends = sends[-16:]
+    for cond, copy in rv_sends:
+        pl.when((g > 0) & cond)(copy.wait_send)
+    sends[-16:] = [((g == 0) & cond, copy) for cond, copy in rv_sends]
     @pl.when((y < 3) & core1)
     def _():
         rv[g, me] = perm[i, 1:3, 0:16]
@@ -208,7 +213,7 @@
             )
     for j in range(LOCAL_HEADS):
         send(lower1, perm.at[j, 1:3, 0:64], r1.at[me], s_p1.at[j], r_1, base + 8 + 2 * j + 1)
-    regroup(g >= 2)
+    regroup(g >= 2, (1,))
 
     head = LOCAL_HEADS * x + i
 
@@ -265,11 +270,14 @@
             line_copy(side, m).start()
             share_mine(side, m).start()
 
-        for b in range(8):
-            pl.when(me != b)(functools.partial(arrived, blocks.at[b, :, 64:128], r_blk.at[1, b]))
+        for m in range(2):
+            arrived(weight(x_far, mine + m), r_wf.at[m])
+            line_copy(2, m).start()
+            share_mine(2, m).start()
         same = position(lane, head) <= position(row, head)
         half = lax.broadcasted_iota(jnp.int32, (64, ROWS), 1) < 64
         for b in range(8):
+            pl.when(me != b)(functools.partial(arrived, blocks.at[b, :, 64:128], r_blk.at[1, b]))
             width = ROWS * (b + 1)
             keys = blocks[0 : b + 1, 1].reshape(width, HEAD_DIM)
             values = blocks[0 : b + 1, 2].reshape(width, HEAD_DIM)
@@ -285,10 +293,6 @@
             hand(b).start()
             ao[b] = (numer[64:] / total[64:]).astype(BF16)
             send_back(b, 64)
-        for m in range(2):
-            arrived(weight(x_far, mine + m), r_wf.at[m])
-            line_copy(2, m).start()
-            share_mine(2, m).start()
         take_theirs(0)
         take_theirs(1)
 
@@ -326,16 +330,13 @@
             to_line(y == 1, 2, pack.at[h], rp.at[1, h], r_y.at[1])
 
         for h in range(4):
-            later = (y < 3) & (g <= h)
+            later = (y < 3) & ((g <= h) | (upper1 & (g == h + 1)))
             arrived_if(later & (g != h), rv.at[h], r_v.at[h])
             arrived_if(later & (g == h), rv.at[h, 0:7], r_v.at[h])
             pass_on(later, h, rv.at[h])
         for h in range(2):
             arrived_if(upper2, r2.at[h], r_2.at[h])
             pass_on(upper2, h, r2.at[h, :, :, 0:16])
-        arrived_if(upper1, r1, r_1)
-        for h in (0, 2):
-            pass_on(g == h + 1, h, r1.at[:, :, 0:16])
 
         for b in range(8):
             arrived(pre.at[b], r_pre.at[b])
@@ -396,18 +397,20 @@
         def level_rows(ref, n, w, rows):
             return ref[..., n, 0:w, :].reshape(rows, HEAD_DIM)
 
+        @pl.when(upper2)
+        def _():
+            update(32, level_rows(r2, 0, 32, 512), level_rows(r2, 1, 32, 512))
+            keys, values = level_rows(r2, 0, 16, 256), level_rows(r2, 1, 16, 256)
+            update(16, keys, values)
+            update(16, keys, values, thin)
+
+        arrived_if(upper1, r1, r_1)
+
         @pl.when(upper1)
         def _():
             update(64, level_rows(r1, 0, 64, 512), level_rows(r1, 1, 64, 512))
             update(32, level_rows(r1, 0, 32, 256), level_rows(r1, 1, 32, 256))
             keys, values = level_rows(r1, 0, 16, 128), level_rows(r1, 1, 16, 128)
-            update(16, keys, values)
-            update(16, keys, values, thin)
-
-        @pl.when(upper2)
-        def _():
-            update(32, level_rows(r2, 0, 32, 512), level_rows(r2, 1, 32, 512))
-            keys, values = level_rows(r2, 0, 16, 256), level_rows(r2, 1, 16, 256)
             update(16, keys, values)
             update(16, keys, values, thin)
 
@@ -441,6 +444,9 @@
         for cond, copy in passes:
             pl.when(cond)(copy.wait_send)
 
+    def quarter(x_):
+        return pl.ds(pl.multiple_of(32 * x_, 32), 32)
+
     for j in range(LOCAL_HEADS):
         for half in range(2):
             sender = 2 * j + (1 - half)
@@ -448,26 +454,23 @@
                 functools.partial(arrived, att.at[j, 64 * half : 64 * half + 64], r_att.at[j, half])
             )
         pick = jnp.where(row == position(lane, LOCAL_HEADS * x + j), 1.0, 0.0).astype(BF16)
-        nat[:, j * HEAD_DIM : (j + 1) * HEAD_DIM] = dot(pick, att[j]).astype(BF16)
-
-    def quarter(x_):
-        return pl.ds(pl.multiple_of(32 * x_, 32), 32)
-
-    for d in (2, 1, 3):
-        there = lax.rem(x + d, X)
-        send(None, nat.at[quarter(there)], ax.at[x], s_ax.at[d - 1], r_ax.at[d - 1], s, there)
+        nat[j] = dot(pick, att[j]).astype(BF16)
+        for d in (2, 1, 3):
+            there = lax.rem(x + d, X)
+            send(None, nat.at[j, quarter(there)], ax.at[x, j], s_ax.at[d - 1, j], r_ax.at[d - 1], s, there)
 
     pl.when(core0)(functools.partial(take_theirs, 2))
 
     for d in (0, 1, 3, 2):
         there = lax.rem(x + X - d, X)
         if d == 0:
-            rows = nat[quarter(x)]
+            rows = nat[:, quarter(x)]
         else:
             arrived(ax.at[there], r_ax.at[d - 1])
             rows = ax[there]
             n = {1: 0, 3: 1, 2: 2}[d]
             pl.when(core1)(functools.partial(arrived, w_ref.at[there], r_ws.at[n]))
+        rows = jnp.concatenate([rows[j] for j in range(LOCAL_HEADS)], axis=1)
         for n in range(D // COLS):
             cols = slice(n * COLS, (n + 1) * COLS)
             product = dot(rows, w_ref[there, :, cols])
@@ -523,13 +526,13 @@
             pltpu.VMEM((8, 64, hd), F32),
             pltpu.VMEM((8, 64, hd), BF16),
             pltpu.VMEM((LOCAL_HEADS, ROWS, hd), BF16),
-            pltpu.VMEM((ROWS, LOCAL_HEADS * hd), BF16),
-            pltpu.VMEM((X, ROWS // X, LOCAL_HEADS * hd), BF16),
+            pltpu.VMEM((LOCAL_HEADS, ROWS, hd), BF16),
+            pltpu.VMEM((X, LOCAL_HEADS, ROWS // X, hd), BF16),
             pltpu.VMEM((X, LOCAL_HEADS * hd, D), BF16),
             pltpu.VMEM((ROWS // X, D), F32),
             pltpu.SemaphoreType.REGULAR,
             dma((3,)), dma, dma((4,)), dma((2, 4)), dma((4, 4)), dma((2, 4)), dma((8,)), dma((3, 4)),
-            dma((8,)), dma((8,)), dma((X - 1,)), dma((2, 2)), dma((2,)), dma((3, 2)), dma((3, 4)),
+            dma((8,)), dma((8,)), dma((X - 1, 4)), dma((2, 2)), dma((2,)), dma((3, 2)), dma((3, 4)),
             dma((2, 8)), dma((8,)), dma, dma((2,)), dma((4,)), dma((3,)), dma((8,)), dma((4, 2)),
             dma((X - 1,)), dma((2, 2)), dma((2,)), dma((3, 2)), dma((3,)),
         ],

time: 51.2 us -> 49.1 us (0.959)
  the two profiles are of different devices: /device:TPU:488 before, /device:TPU:17 now
where the time goes in v4:
time: 49.1 us; the launch traced here: 48.9 us
  Pallas kernels  47.4 us (97%)
  local copies, waits for them, and re-layouts  1.57 us (3%)
    pallas_call x1, Pallas kernels, per_device(): pl.pallas_call(kernel, out_shape=jax.ShapeDtypeStruct((ROWS // X, D), BF1...  47.4 us
    unnamed x1, local copies, waits for them, and re-layouts  1.57 us

profile of v4, /device:TPU:17, one launch (start us, length us, event | category | flops | bytes accessed | tf_op | source)
XLA Modules:
  0.0 48.9 jit_solution(12353762802898746557)
XLA Ops:
  0.0 47.4 %shard_map.46 = bf16[32,2048]{1,0:T(8,128)(2,1)} custom-call(bf16[128,512]{1,0:T(8,128)(2,1)} %q_hbm.1, bf16[128,512]{1,0:T(8,128)(2,1)} %k_hbm.1, bf16[128,512]{1,0:T(8,128)(2,1)} %v_hbm.1, bf16[512,2048]{1,0:T(8,128)(2,1)} %w_hbm.1), custom_call_target="tpu_custom_call" | custom-call | tf_op jit(solution)/shard_map/pallas_call | solution.py:504
  47.4 1.6 %copy.6 = bf16[32,2048]{1,0:T(8,128)(2,1)} copy(bf16[32,2048]{1,0:T(8,128)(2,1)} %shard_map.46) | data formatting | bytes 262144

commit v5 on v4

--- a/solution.py
+++ b/solution.py
@@ -25,6 +25,10 @@
 
 def dot_t(a, b):
     return lax.dot_general(a, b, (((1,), (1,)), ((), ())), preferred_element_type=F32)
+
+def levels(r):
+    return sum(jnp.where(r < n, 1, 0) for n in (64, 32, 16, 8))
+
 
 def position(r, h):
     return jnp.where(
@@ -244,7 +248,7 @@
 
         def forward(b):
             return pltpu.make_async_remote_copy(
-                src_ref=blocks.at[b, :, 0:64], dst_ref=pre.at[b], send_sem=s_fwd.at[b], recv_sem=r_pre.at[b],
+                src_ref=blocks.at[b, 0, 0:64], dst_ref=pre.at[b], send_sem=s_fwd.at[b], recv_sem=r_pre.at[b],
                 device_id=(s + 1, x), device_id_type=MESH,
             )
 
@@ -275,6 +279,7 @@
             line_copy(2, m).start()
             share_mine(2, m).start()
         same = position(lane, head) <= position(row, head)
+        times = (1 + jnp.minimum(levels(row), levels(lane))).astype(F32)
         half = lax.broadcasted_iota(jnp.int32, (64, ROWS), 1) < 64
         for b in range(8):
             pl.when(me != b)(functools.partial(arrived, blocks.at[b, :, 64:128], r_blk.at[1, b]))
@@ -285,7 +290,7 @@
             last = jnp.where(same, scores[:, ROWS * b :], NEG)
             scores = last if b == 0 else jnp.concatenate([scores[:, : ROWS * b], last], axis=1)
             peak = jnp.max(scores, axis=1, keepdims=True)
-            weights = jnp.exp2(scores - peak)
+            weights = jnp.exp2(scores - peak) * jnp.concatenate([times] * (b + 1), axis=1)
             total = jnp.sum(weights, axis=1, keepdims=True)
             numer = dot(weights.astype(BF16), values)
             stat[b, 0] = numer[:64]
@@ -341,92 +346,62 @@
         for b in range(8):
             arrived(pre.at[b], r_pre.at[b])
 
-        def update(w, keys, values, mask=None, first=False, roll=False):
+        top[...] = jnp.full_like(top, NEG)
+        den[...] = jnp.zeros_like(den)
+        num[...] = jnp.zeros_like(num)
+
+        def update(w, keys, values, packed=False):
             nb = ROWS // w
+            shape = (ROWS, keys.shape[0])
+            r_query = lax.rem(lax.broadcasted_iota(jnp.int32, shape, 0), w)
+            r_key = lax.rem(lax.broadcasted_iota(jnp.int32, shape, 1), w)
+            if packed:
+                both = (r_query < 8) & (r_key < 8)
+                count = jnp.where(both, 1.0, 0.0)
+            else:
+                count = (jnp.minimum(levels(r_query), levels(r_key)) - {64: 0, 32: 1, 16: 2}[w]).astype(F32)
             for b0 in range(0, 8, nb):
                 at = (slice(b0, b0 + nb), slice(0, w))
-                query = pre[b0 : b0 + nb, 0, 0:w].reshape(ROWS, HEAD_DIM)
+                query = pre[b0 : b0 + nb, 0:w].reshape(ROWS, HEAD_DIM)
                 scores = dot_t(query, keys) * SCALE
-                if mask is not None:
-                    scores = jnp.where(mask(b0 * w, scores.shape), scores, NEG)
-                peak = jnp.max(scores, axis=1, keepdims=True)
-                if first:
-                    peak = jnp.broadcast_to(peak, (ROWS, HEAD_DIM))
-                else:
-                    was = top[at].reshape(ROWS, HEAD_DIM)
-                    peak = jnp.maximum(was, peak)
-                    keep = jnp.exp2(was - peak)
-                weights = jnp.exp2(scores - peak[:, :1])
-                total = jnp.sum(weights, axis=1, keepdims=True)
-                if roll:
+                if packed:
+                    scores = jnp.where(both, scores, NEG)
+                was = top[at].reshape(ROWS, HEAD_DIM)
+                peak = jnp.maximum(was, jnp.max(scores, axis=1, keepdims=True))
+                keep = jnp.exp2(was - peak)
+                weights = jnp.exp2(scores - peak[:, :1]) * count
+                total = jnp.sum(weights, axis=1, keepdims=True) + den[at].reshape(ROWS, HEAD_DIM) * keep
+                if packed:
                     weights = pltpu.roll(weights, 8, axis=1)
-                numer = dot(weights.astype(BF16), values)
-                if first:
-                    total = jnp.broadcast_to(total, (ROWS, HEAD_DIM))
-                else:
-                    total = total + den[at].reshape(ROWS, HEAD_DIM) * keep
-                    numer = numer + num[at].reshape(ROWS, HEAD_DIM) * keep
+                numer = dot(weights.astype(BF16), values) + num[at].reshape(ROWS, HEAD_DIM) * keep
                 top[at] = peak.reshape(nb, w, HEAD_DIM)
                 den[at] = total.reshape(nb, w, HEAD_DIM)
                 num[at] = numer.reshape(nb, w, HEAD_DIM)
 
-        def place(n, w):
-            return n // w * ROWS + position(lax.rem(n, w), head)
-
-        def causal(w, start, shape):
-            query = start + lax.broadcasted_iota(jnp.int32, shape, 0)
-            key = lax.broadcasted_iota(jnp.int32, shape, 1)
-            return place(key, w) <= place(query, w)
-
-        def thin(start, shape):
-            query = lax.broadcasted_iota(jnp.int32, shape, 0)
-            key = lax.broadcasted_iota(jnp.int32, shape, 1)
-            return (lax.rem(query, 16) < 8) & (lax.rem(key, 16) < 8)
-
-        def thin_causal(start, shape):
-            return thin(start, shape) & causal(16, start, shape)
-
-        def own(n, w):
-            return pre[:, n, 0:w].reshape(8 * w, HEAD_DIM)
-
-        update(64, own(1, 64), own(2, 64), functools.partial(causal, 64), first=True)
-        update(32, own(1, 32), own(2, 32), functools.partial(causal, 32))
-        update(16, own(1, 16), own(2, 16), functools.partial(causal, 16))
-        update(16, own(1, 16), own(2, 16), thin_causal)
-
         def level_rows(ref, n, w, rows):
             return ref[..., n, 0:w, :].reshape(rows, HEAD_DIM)
 
         @pl.when(upper2)
         def _():
             update(32, level_rows(r2, 0, 32, 512), level_rows(r2, 1, 32, 512))
-            keys, values = level_rows(r2, 0, 16, 256), level_rows(r2, 1, 16, 256)
-            update(16, keys, values)
-            update(16, keys, values, thin)
 
         arrived_if(upper1, r1, r_1)
 
         @pl.when(upper1)
         def _():
             update(64, level_rows(r1, 0, 64, 512), level_rows(r1, 1, 64, 512))
-            update(32, level_rows(r1, 0, 32, 256), level_rows(r1, 1, 32, 256))
-            keys, values = level_rows(r1, 0, 16, 128), level_rows(r1, 1, 16, 128)
-            update(16, keys, values)
-            update(16, keys, values, thin)
 
         @pl.when(y >= 2)
         def _():
             for t in range(2):
                 arrived(rp.at[t], r_y.at[t])
-            both = rp[...].reshape(1024, HEAD_DIM)
-            update(16, both, both, thin, roll=True)
+            tiles = rp[...].reshape(1024, HEAD_DIM)
+            update(16, tiles, tiles, packed=True)
 
         @pl.when(lax.rem(y, 2) == 1)
         def _():
             arrived(ry, r_y.at[2])
-            keys, values = ry[:, :, 0].reshape(512, HEAD_DIM), ry[:, :, 1].reshape(512, HEAD_DIM)
-            update(16, keys, values)
-            update(16, keys, values, thin)
+            update(16, ry[:, :, 0].reshape(512, HEAD_DIM), ry[:, :, 1].reshape(512, HEAD_DIM))
 
         for b in range(8):
             arrived(l0.at[b], r_l0.at[b])
@@ -512,7 +487,7 @@
             pltpu.VMEM((ROWS, LOCAL_HEADS * hd), BF16),
             pltpu.VMEM((LOCAL_HEADS, 3, ROWS, hd), BF16),
             pltpu.VMEM((8, 3, ROWS, hd), BF16),
-            pltpu.VMEM((8, 3, 64, hd), BF16),
+            pltpu.VMEM((8, 64, hd), BF16),
             pltpu.VMEM((8, 2, 64, hd), BF16),
             pltpu.VMEM((2, 8, 2, 32, hd), BF16),
             pltpu.VMEM((4, 8, 2, 16, hd), BF16),

time: 49.1 us -> 49.1 us (level)
  no operation moved by 1% of the time
where the time goes in v5:
time: 49.1 us; the launch traced here: 48.9 us
  Pallas kernels  47.4 us (97%)
  local copies, waits for them, and re-layouts  1.57 us (3%)
    pallas_call x1, Pallas kernels, per_device(): pl.pallas_call(kernel, out_shape=jax.ShapeDtypeStruct((ROWS // X, D), BF1...  47.4 us
    unnamed x1, local copies, waits for them, and re-layouts  1.57 us

profile of v5, /device:TPU:17, one launch (start us, length us, event | category | flops | bytes accessed | tf_op | source)
XLA Modules:
  0.0 48.9 jit_solution(3537039747820972440)
XLA Ops:
  0.0 47.4 %shard_map.46 = bf16[32,2048]{1,0:T(8,128)(2,1)} custom-call(bf16[128,512]{1,0:T(8,128)(2,1)} %q_hbm.1, bf16[128,512]{1,0:T(8,128)(2,1)} %k_hbm.1, bf16[128,512]{1,0:T(8,128)(2,1)} %v_hbm.1, bf16[512,2048]{1,0:T(8,128)(2,1)} %w_hbm.1), custom_call_target="tpu_custom_call" | custom-call | tf_op jit(solution)/shard_map/pallas_call | solution.py:479
  47.4 1.6 %copy.6 = bf16[32,2048]{1,0:T(8,128)(2,1)} copy(bf16[32,2048]{1,0:T(8,128)(2,1)} %shard_map.46) | data formatting | bytes 262144

commit v6 on v5

--- a/solution.py
+++ b/solution.py
@@ -300,6 +300,7 @@
             send_back(b, 64)
         take_theirs(0)
         take_theirs(1)
+        pl.when(g == 0)(functools.partial(take_theirs, 2))
 
         for b in range(8):
             forward(b).wait_send()
@@ -434,7 +435,7 @@
             there = lax.rem(x + d, X)
             send(None, nat.at[j, quarter(there)], ax.at[x, j], s_ax.at[d - 1, j], r_ax.at[d - 1], s, there)
 
-    pl.when(core0)(functools.partial(take_theirs, 2))
+    pl.when(core0 & (g > 0))(functools.partial(take_theirs, 2))
 
     for d in (0, 1, 3, 2):
         there = lax.rem(x + X - d, X)

time: 49.1 us -> 49 us (level)
  no operation moved by 1% of the time
where the time goes in v6:
time: 49 us; the launch traced here: 48.9 us
  Pallas kernels  47.3 us (97%)
  local copies, waits for them, and re-layouts  1.57 us (3%)
    pallas_call x1, Pallas kernels, per_device(): pl.pallas_call(kernel, out_shape=jax.ShapeDtypeStruct((ROWS // X, D), BF1...  47.3 us
    unnamed x1, local copies, waits for them, and re-layouts  1.57 us

profile of v6, /device:TPU:17, one launch (start us, length us, event | category | flops | bytes accessed | tf_op | source)
XLA Modules:
  0.0 48.9 jit_solution(13430443365298346840)
XLA Ops:
  0.0 47.3 %shard_map.46 = bf16[32,2048]{1,0:T(8,128)(2,1)} custom-call(bf16[128,512]{1,0:T(8,128)(2,1)} %q_hbm.1, bf16[128,512]{1,0:T(8,128)(2,1)} %k_hbm.1, bf16[128,512]{1,0:T(8,128)(2,1)} %v_hbm.1, bf16[512,2048]{1,0:T(8,128)(2,1)} %w_hbm.1), custom_call_target="tpu_custom_call" | custom-call | tf_op jit(solution)/shard_map/pallas_call | solution.py:480
  47.3 1.6 %copy.6 = bf16[32,2048]{1,0:T(8,128)(2,1)} copy(bf16[32,2048]{1,0:T(8,128)(2,1)} %shard_map.46) | data formatting | bytes 262144
